TPU v7x, 256 devices: a whole 4x4x8 slice. The times are simulated.
256 devices in a mesh: dp: 16 (over z, core), node: 16 (over y, x).
Axes of the slice: x: 4, y: 4, z: 8, core: 2. Of those that a mesh axis runs over, the one named last changes fastest.
Arguments:
- node_state: bfloat16 [131072, 1024], P(('dp', 'node')), parts along dimension 0, may hold values from -6 to 6
- edge_recv: int32 [1048576], P(('dp', 'node')), parts along dimension 0, may hold values from 0 to 511
- edge_send: int32 [1048576], P(('dp', 'node')), parts along dimension 0, may hold values from 0 to 2559
- halo_rows: int32 [256, 16, 128], P(('dp', 'node')), parts along dimension 0, may hold values from 0 to 511
- window_reach: int32 [16], replicated, may hold values from 32 to 128
- w_recv: bfloat16 [1024, 512], replicated, may hold values from -0.1875 to 0.1875
- w_send: bfloat16 [1024, 512], replicated, may hold values from -0.1875 to 0.1875
- edge_bias: float32 [512], replicated, may hold values from -4 to 4
- w_message: bfloat16 [512, 512], replicated, may hold values from -0.25 to 0.25
- msg_gain: float32 [512], replicated, may hold values from 0.5 to 2
- w_lift: bfloat16 [512, 1024], replicated, may hold values from -0.25 to 0.25
- attn_gain: float32 [1024], replicated, may hold values from 0.5 to 2
- w_qkv: bfloat16 [1024, 16, 192], replicated, may hold values from -1 to 1
- w_out: bfloat16 [1024, 1024], replicated, may hold values from -0.1875 to 0.1875
Outputs:
- result: bfloat16 [131072, 1024], P(('dp', 'node')), parts along dimension 0
There are 16 independent parts, one for each index of `dp`. A program takes and returns all parts, laid end to end along the dimension named above; an argument that names none is the same for every part. Nothing has to cross between parts.
All inputs are finite; a program needn't handle non-finite values.
Results may differ from a plain program's by a relative error of at most 0.0085.
Values may be sent and summed in bfloat16 or wider, within the bound.
No kernel may reach another device: no remote copies, remote signals or barrier semaphores. Data moves between devices by JAX's collectives and lax.ppermute only.
A program may use at most 128 MiB of HBM per device.

v0:
```python
import jax
import jax.numpy as jnp
from jax import lax
from jax.sharding import PartitionSpec as P

WIN_MAX = 128


def rms_scale(values, gain):
    mean_sq = jnp.mean(values * values, axis=-1, keepdims=True)
    return values * lax.rsqrt(mean_sq + 1e-05) * gain


def attend(query, keys, values, reach, q_start, k_start, total):
    q_pos = q_start + jnp.arange(query.shape[0], dtype=jnp.int32)
    k_pos = k_start + jnp.arange(keys.shape[0], dtype=jnp.int32)
    apart = jnp.abs(q_pos[:, None] - k_pos[None, :])
    inside = (k_pos >= 0) & (k_pos < total)
    valid = (apart[None, :, :] <= reach[:, None, None]) & inside[None, None, :]
    score = jnp.einsum(
        "qhd,khd->hqk", query, keys, preferred_element_type=jnp.float32
    ) * query.shape[2] ** (-0.5)
    score = jnp.where(valid, score, -1e30)
    top = jnp.max(score, axis=-1, keepdims=True)
    expo = jnp.where(valid, jnp.exp(score - top), 0.0)
    weights = (expo / jnp.sum(expo, axis=-1, keepdims=True)).astype(jnp.bfloat16)
    mixed = jnp.einsum("hqk,khd->qhd", weights, values, preferred_element_type=jnp.float32)
    return mixed.astype(jnp.bfloat16)


def local(
    node_state,
    edge_recv,
    edge_send,
    halo_rows,
    window_reach,
    w_recv,
    w_send,
    edge_bias,
    w_message,
    msg_gain,
    w_lift,
    attn_gain,
    w_qkv,
    w_out,
):
    rows = node_state.shape[0]
    hidden = w_recv.shape[1]
    peers = halo_rows.shape[1]
    halo = halo_rows.shape[2]
    recv_proj = jnp.dot(node_state, w_recv, preferred_element_type=jnp.float32).astype(jnp.bfloat16)
    send_proj = jnp.dot(node_state, w_send, preferred_element_type=jnp.float32).astype(jnp.bfloat16)
    outgoing = jnp.take(send_proj, halo_rows.reshape(-1), axis=0).reshape(peers, halo, hidden)
    incoming = lax.all_to_all(outgoing, "node", split_axis=0, concat_axis=0, tiled=True)
    table = jnp.concatenate([send_proj, incoming.reshape(peers * halo, hidden)], axis=0)
    pre = (
        jnp.take(recv_proj, edge_recv, axis=0).astype(jnp.float32)
        + jnp.take(table, edge_send, axis=0).astype(jnp.float32)
        + edge_bias
    )
    message = jax.nn.silu(pre).astype(jnp.bfloat16)
    mixed = jnp.dot(message, w_message, preferred_element_type=jnp.float32).astype(jnp.bfloat16)
    onehot = (jnp.arange(rows, dtype=jnp.int32)[:, None] == edge_recv[None, :]).astype(jnp.bfloat16)
    aggregate = jnp.dot(onehot, mixed, preferred_element_type=jnp.float32)
    normed = rms_scale(aggregate, msg_gain).astype(jnp.bfloat16)
    state = (
        node_state.astype(jnp.float32) + jnp.dot(normed, w_lift, preferred_element_type=jnp.float32)
    ).astype(jnp.bfloat16)
    attn_in = rms_scale(state.astype(jnp.float32), attn_gain).astype(jnp.bfloat16)
    qkv = jnp.einsum("rd,dhc->rhc", attn_in, w_qkv, preferred_element_type=jnp.float32).astype(
        jnp.bfloat16
    )
    width = qkv.shape[2] // 3
    total = rows * lax.axis_size("node")
    owned = lax.all_to_all(qkv, "node", split_axis=1, concat_axis=0, tiled=True)
    per_dev = owned.shape[1]
    reach = lax.dynamic_slice_in_dim(window_reach, lax.axis_index("node") * per_dev, per_dev)
    query = owned[:, :, :width]
    padded = jnp.pad(owned[:, :, width:], ((WIN_MAX, WIN_MAX), (0, 0), (0, 0)))
    block = min(512, total)

    def one_block(index):
        start = index * block
        q_part = lax.dynamic_slice_in_dim(query, start, block, 0)
        kv_part = lax.dynamic_slice_in_dim(padded, start, block + 2 * WIN_MAX, 0)
        return attend(
            q_part,
            kv_part[:, :, :width],
            kv_part[:, :, width:],
            reach,
            start,
            start - WIN_MAX,
            total,
        )

    blocks = lax.map(one_block, jnp.arange(total // block, dtype=jnp.int32))
    head_out = blocks.reshape(total, per_dev, width)
    attended = lax.all_to_all(head_out, "node", split_axis=0, concat_axis=1, tiled=True)
    flat = attended.reshape(rows, -1)
    result = state.astype(jnp.float32) + jnp.dot(flat, w_out, preferred_element_type=jnp.float32)
    return result.astype(jnp.bfloat16)


def solution(mesh):
    in_specs = (
        P(("dp", "node"), None),
        P(("dp", "node")),
        P(("dp", "node")),
        P(("dp", "node"), None, None),
        P(),
        P(),
        P(),
        P(),
        P(),
        P(),
        P(),
        P(),
        P(),
        P(),
    )
    out_specs = P(("dp", "node"), None)
    return jax.shard_map(local, mesh=mesh, in_specs=in_specs, out_specs=out_specs, check_vma=False)
```

profile of v0, /device:TPU:224, one launch (start us, length us, event | category | flops | bytes accessed | tf_op | source)
XLA Modules:
  0.0 407.6 jit_solution(14726991738126672607)
XLA Ops:
  1.6 2.2 convolution_convert_fusion.2
  3.8 9.2 %gather_fusion.1 = bf16[2048,512]{1,0:T(8,128)(2,1)} fusion(bf16[512,512]{1,0:T(8,128)(2,1)S(1)} %convolution_convert_fusion.2, s32[2048]{0:T(1024)S(1)} %broadcast_clamp_fusion), kind=kCustom, calls=%fused_computation.1 | custom fusion | bytes 4202496 | tf_op jit(solution)/shard_map/jit(_take)/gather | solution.py:53
  13.0 2.8 broadcast_select_fusion
  15.8 7.2 %all-to-all-start = ((bf16[16,128,512]{2,1,0:T(8,128)(2,1)}), bf16[16,128,512]{2,1,0:T(8,128)(2,1)}, u32[]{:S(2)}, u32[]{:S(2)}) async-start(bf16[16,128,512]{2,1,0:T(8,128)(2,1)} %broadcast_select_fusion), calls=%async_computation | async-start | bytes 4194304 | tf_op jit(solution)/shard_map/all_to_all | solution.py:54
  23.0 2.2 convolution_convert_fusion.3
  25.3 17.3 %gather_fusion = bf16[4096,512]{1,0:T(8,128)(2,1)} fusion(bf16[512,512]{1,0:T(8,128)(2,1)S(1)} %convolution_convert_fusion.3, s32[4096]{0:T(1024)S(1)} %fusion.25), kind=kCustom, calls=%fused_computation | custom fusion | bytes 8404992 | tf_op jit(solution)/shard_map/jit(_take)/gather | solution.py:57
  42.6 12.1 %all-to-all-done = bf16[16,128,512]{2,1,0:T(8,128)(2,1)} async-done(((bf16[16,128,512]{2,1,0:T(8,128)(2,1)}), bf16[16,128,512]{2,1,0:T(8,128)(2,1)}, u32[]{:S(2)}, u32[]{:S(2)}) %all-to-all-start) | async-done | bytes 2097184 | tf_op jit(solution)/shard_map/all_to_all | solution.py:54
  54.7 3.3 pad_maximum_fusion
  58.0 19.6 %gather_fusion.2 = bf16[4096,512]{1,0:T(8,128)(2,1)} fusion(bf16[2560,512]{1,0:T(8,128)(2,1)} %pad_maximum_fusion, s32[4096]{0:T(1024)S(1)} %fusion.26), kind=kCustom, calls=%fused_computation.2 | custom fusion | bytes 8404992 | tf_op jit(solution)/shard_map/jit(_take)/gather | solution.py:58
  77.6 11.3 %multiply_reduce_fusion = (f32[512]{0:T(512)S(1)}, f32[512,512]{0,1:T(8,128)}) fusion(bf16[512,512]{1,0:T(8,128)(2,1)S(1)} %copy-done.4, f32[512]{0:T(512)S(1)} %copy-done.6, bf16[4096,512]{1,0:T(8,128)(2,1)} %gather_fusion.2, bf16[4096,512]{1,0:T(8,128)(2,1)} %gather_fusion, pred[4096]{0:T(1024)(128)(4,1)S(1)} %get-tuple-element.101, ...), kind=kOutput, calls=%fused_computation.46 | convolution fusion | flops 4322754048 | bytes 9990144 | tf_op jit(solution)/shard_map/dot_general | solution.py:64
  88.9 2.8 fusion.14
  91.8 6.2 %fusion.19 = f32[512,3072]{0,1:S(1)} fusion(bf16[1024,3072]{0,1:T(8,128)(2,1)} %bitcast.81, bf16[512,1024]{1,0:T(8,128)(2,1)S(1)} %get-tuple-element.100, f32[1024]{0:T(1024)S(1)} %copy-done.5, f32[512]{0:T(512)S(1)} %add_rsqrt_fusion), kind=kOutput, calls=%fused_computation.42 | convolution fusion | flops 3223322624 | bytes 13637632
  98.0 2.1 convert_element_type.73
  100.1 4.8 %all-to-all-start.1 = ((bf16[512,16,192]{0,2,1:T(8,128)(2,1)}), bf16[512,16,192]{0,2,1:T(8,128)(2,1)}, u32[]{:S(2)}, u32[]{:S(2)}) async-start(bf16[512,16,192]{0,2,1:T(8,128)(2,1)} %convert_element_type.73), calls=%async_computation.1 | async-start | bytes 6291456 | tf_op jit(solution)/shard_map/all_to_all | solution.py:75
  105.6 43.1 %all-to-all-done.1 = bf16[512,16,192]{0,2,1:T(8,128)(2,1)} async-done(((bf16[512,16,192]{0,2,1:T(8,128)(2,1)}), bf16[512,16,192]{0,2,1:T(8,128)(2,1)}, u32[]{:S(2)}, u32[]{:S(2)}) %all-to-all-start.1) | async-done | bytes 3145760 | tf_op jit(solution)/shard_map/all_to_all | solution.py:75
  148.7 2.3 copy.25
  152.2 1.5 pad.4
  153.7 147.0 %while.12 = (s32[]{:T(128)}, bf16[16,512,1,64]{1,3,2,0:T(8,128)(2,1)S(1)}, s32[16]{0:T(128)S(1)}, bf16[8448,1,128]{0,2,1:T(8,128)(2,1)}, s32[1]{0:T(128)}, /*ind...) while((s32[]{:T(128)}, ...), condition=%wide.region_5.6_spmd, body=%wide.region_2.5_spmd.sunk | while | flops 109350152 | bytes 11374628 | solution.py:96
  154.9 2.3 fusion.44
  159.9 3.0 fusion.46
  164.1 2.3 fusion.44
  169.1 3.0 fusion.46
  173.2 2.3 fusion.44
  176.7 1.5 fusion.45
  178.2 3.0 fusion.46
  182.4 2.3 fusion.44
  187.4 3.0 fusion.46
  191.6 2.3 fusion.44
  195.1 1.5 fusion.45
  196.6 3.0 fusion.46
  200.8 2.3 fusion.44
  204.3 1.5 fusion.45
  205.8 3.0 fusion.46
  210.0 2.3 fusion.44
  215.0 3.0 fusion.46
  219.2 2.3 fusion.44
  222.7 1.5 fusion.45
  224.2 3.0 fusion.46
  228.4 2.3 fusion.44
  233.4 3.0 fusion.46
  237.6 2.3 fusion.44
  242.6 3.0 fusion.46
  246.7 2.3 fusion.44
  251.7 3.0 fusion.46
  255.9 2.3 fusion.44
  260.9 3.0 fusion.46
  265.1 2.3 fusion.44
  268.6 1.5 fusion.45
  270.1 3.0 fusion.46
  274.3 2.3 fusion.44
  279.3 3.0 fusion.46
  283.5 2.3 fusion.44
  287.0 1.5 fusion.45
  288.5 3.0 fusion.46
  292.7 2.3 fusion.44
  297.7 3.0 fusion.46
  300.7 1.8 copy.23
  302.5 12.5 %reshape.190 = bf16[8192,1,64]{2,1,0:T(2,128)(2,1)} reshape(bf16[16,512,1,64]{3,1,0,2:T(8,128)(2,1)} %copy.23) | data formatting | bytes 2097152 | tf_op jit(solution)/shard_map/reshape | solution.py:97
  315.6 46.5 %reduce.10 = bf16[8192,64]{1,0:T(8,128)(2,1)} reduce(bf16[8192,1,64]{2,1,0:T(2,128)(2,1)} %reshape.190, bf16[]{:T(256)} %broadcast.166), dimensions={1}, to_apply=%reshape.190.reduce_sub_computation | reduce | bytes 2097154 | tf_op jit(solution)/shard_map/reshape | solution.py:97
  362.1 3.9 reshape.191
  366.0 19.8 %all_to_all.38 = bf16[16,2,16384]{2,1,0:T(2,128)(2,1)} all-to-all(bf16[16,2,16384]{2,1,0:T(2,128)(2,1)S(1)} %reshape.191), channel_id=1, replica_groups=mesh['dp'=16,'node'=16] {'node'}, dimensions={0} | all-to-all | bytes 2097152 | tf_op jit(solution)/shard_map/all_to_all | solution.py:98
  385.8 10.1 %reshape.192 = bf16[8192,1,64]{2,1,0:T(2,128)(2,1)} reshape(bf16[16,2,16384]{2,1,0:T(2,128)(2,1)} %all_to_all.38) | data formatting | bytes 2097152
  395.9 8.2 %copy.21 = bf16[8192,1,64]{0,2,1:T(8,128)(2,1)S(1)} copy(bf16[8192,1,64]{2,1,0:T(2,128)(2,1)} %reshape.192) | data formatting | bytes 2097152 | tf_op jit(solution)/shard_map/all_to_all | solution.py:98
  405.3 2.3 fusion.17
  (142 shorter events, 48.0 us)
Async XLA Ops:
  0.0 405.0 %copy-start = (bf16[1024,1024]{1,0:T(8,128)(2,1)S(1)}, bf16[1024,1024]{1,0:T(8,128)(2,1)}, u32[]{:S(2)}) copy-start(bf16[1024,1024]{1,0:T(8,128)(2,1)} %param.29) | copy-start | bytes 6291460
  15.8 7.2 %copy-start.3 = (s32[4096]{0:T(1024)S(1)}, s32[4096]{0:T(1024)}, u32[]{:S(2)}) copy-start(s32[4096]{0:T(1024)} %param.17) | copy-start | bytes 49156
  15.8 38.9 %all-to-all-start = ((bf16[16,128,512]{2,1,0:T(8,128)(2,1)}), bf16[16,128,512]{2,1,0:T(8,128)(2,1)}, u32[]{:S(2)}, u32[]{:S(2)}) async-start(bf16[16,128,512]{2,1,0:T(8,128)(2,1)} %broadcast_select_fusion), calls=%async_computation | async-start | bytes 4194304 | tf_op jit(solution)/shard_map/all_to_all | solution.py:54
  25.3 17.3 %copy-start.2 = (s32[4096]{0:T(1024)S(1)}, s32[4096]{0:T(1024)}, u32[]{:S(2)}) copy-start(s32[4096]{0:T(1024)} %param.18) | copy-start | bytes 49156
  58.0 19.6 %copy-start.4 = (bf16[512,512]{1,0:T(8,128)(2,1)S(1)}, bf16[512,512]{1,0:T(8,128)(2,1)}, u32[]{:S(2)}) copy-start(bf16[512,512]{1,0:T(8,128)(2,1)} %param.24) | copy-start | bytes 1572868
  58.0 19.6 %copy-start.6 = (f32[512]{0:T(512)S(1)}, f32[512]{0:T(512)}, u32[]{:S(2)}) copy-start(f32[512]{0:T(512)} %param.23) | copy-start | bytes 6148
  77.6 11.3 %copy-start.7 = (f32[512]{0:T(512)S(1)}, f32[512]{0:T(512)}, u32[]{:S(2)}) copy-start(f32[512]{0:T(512)} %param.25) | copy-start | bytes 6148
  88.9 2.8 copy-start.5
  91.8 6.3 %copy-start.9 = (bf16[512,1024]{1,0:T(8,128)(2,1)}, bf16[512,1024]{1,0:T(8,128)(2,1)S(1)}, u32[]{:S(2)}) copy-start(bf16[512,1024]{1,0:T(8,128)(2,1)S(1)} %get-tuple-element.100) | copy-start | bytes 3145732
  100.1 4.8 %copy-start.8 = (s32[16]{0:T(128)S(1)}, s32[16]{0:T(128)}, u32[]{:S(2)}) copy-start(s32[16]{0:T(128)} %param.20) | copy-start | bytes 196
  100.1 48.6 %all-to-all-start.1 = ((bf16[512,16,192]{0,2,1:T(8,128)(2,1)}), bf16[512,16,192]{0,2,1:T(8,128)(2,1)}, u32[]{:S(2)}, u32[]{:S(2)}) async-start(bf16[512,16,192]{0,2,1:T(8,128)(2,1)} %convert_element_type.73), calls=%async_computation.1 | async-start | bytes 6291456 | tf_op jit(solution)/shard_map/all_to_all | solution.py:75
  157.2 1.2 copy-start.1
  166.4 1.2 copy-start.1
  175.6 1.2 copy-start.1
  184.8 1.2 copy-start.1
  194.0 1.2 copy-start.1
  203.1 1.2 copy-start.1
  212.3 1.2 copy-start.1
  221.5 1.2 copy-start.1
  230.7 1.2 copy-start.1
  239.9 1.2 copy-start.1
  249.1 1.2 copy-start.1
  258.3 1.2 copy-start.1
  267.5 1.2 copy-start.1
  276.6 1.2 copy-start.1
  285.8 1.2 copy-start.1
  295.0 1.2 copy-start.1
  404.1 1.2 copy-start.10
where the time goes:
time: 411 us; the launch traced here: 408 us
  local copies, waits for them, and re-layouts  117 us (28%)
  matrix products  113 us (27%)
  other arithmetic  80.6 us (20%)
  waiting for transfers between devices  55.2 us (13%)
  blocking collectives  19.8 us (5%)
  starting transfers between devices  12 us (3%)
  loops' own time  9.71 us (2%)
    dot_general x16, matrix products, attend(): jnp.einsum('hqk,khd->qhd', weights, values, preferred_element_type=jnp.fl...  48.2 us
    reshape x1, other arithmetic, local(): head_out = blocks.reshape(total, per_dev, width)  46.5 us
    all_to_all x1, waiting for transfers between devices, local(): owned = lax.all_to_all(qkv, 'node', split_axis=1, concat_axis=0, tiled=True)  43.1 us
    dot_general x16, matrix products, attend(): jnp.einsum('qhd,khd->hqk', query, keys, preferred_element_type=jnp.float32)  37.4 us
    reduce_sum x16, other arithmetic, attend(): jnp.sum(expo, axis=-1, keepdims=True)  24 us
    all_to_all x1, blocking collectives, local(): lax.all_to_all(head_out, 'node', split_axis=0, concat_axis=1, tiled=True)  19.8 us
    gather x1, local copies, waits for them, and re-layouts, local(): jnp.take(table, edge_send, axis=0).astype(jnp.float32)  19.6 us
    while x32, local copies, waits for them, and re-layouts  18.5 us
  transfers between devices with their start and end apart: 2, of which 2 were waited for; matrix products, arithmetic and copies ran while one was open for 5% of the time, Pallas kernels for 0%

commit v1 on v0

v1 whole, which is shorter than its diff:
```python
import functools

import jax
import jax.numpy as jnp
from jax import lax
from jax.experimental import pallas as pl
from jax.experimental.pallas import tpu as pltpu
from jax.sharding import PartitionSpec as P

WIN = 128
TILE = 256
CHUNK = 256
BIG = 1 << 20
NEG = -1e30
F32 = jnp.float32
BF16 = jnp.bfloat16
VMEM = pl.BlockSpec(memory_space=pltpu.VMEM)
SMEM = pl.BlockSpec(memory_space=pltpu.SMEM)
ANY = pl.BlockSpec(memory_space=pl.ANY)
LIMIT = 44 * 1024 * 1024


def dot(a, b):
    return jnp.dot(a, b, preferred_element_type=F32)


def dot_nt(a, b):
    return lax.dot_general(a, b, (((1,), (1,)), ((), ())), preferred_element_type=F32)


def onehot(index, size):
    place = lax.broadcasted_iota(jnp.int32, (size, index.shape[1]), 0)
    return jnp.where(place == index, 1.0, 0.0).astype(BF16)


def rms_scale(values, gain):
    mean_sq = jnp.mean(values * values, axis=-1, keepdims=True)
    return values * lax.rsqrt(mean_sq + 1e-05) * gain


def send_kernel(x_ref, w_ref, halo_ref, table_ref, out_ref):
    proj = dot(x_ref[...], w_ref[...])
    proj_t = jnp.transpose(proj).astype(BF16)
    for part in range(table_ref.shape[0]):
        table_ref[part] = proj_t[:, part * 128 : (part + 1) * 128]
    rows = x_ref.shape[0]
    for pair in range(out_ref.shape[0] // 2):
        hot = jnp.concatenate(
            [onehot(halo_ref[pl.ds(2 * pair + k, 1), :], rows) for k in range(2)], axis=1
        )
        picked = dot(proj_t, hot).astype(BF16)
        out_ref[2 * pair] = picked[:, :128]
        out_ref[2 * pair + 1] = picked[:, 128:]


def edge_tiles(first, last, ends_ref, keys_ref, table_ref, recv_ref, bias_ref, pre_ref, agg_ref):
    rows = recv_ref.shape[1]

    def chunk_of(index, slot):
        chunk = jnp.concatenate([table_ref[2 * index], table_ref[2 * index + 1]], axis=1)
        return dot(chunk, onehot(slot - index * CHUNK, CHUNK))

    def body(tile, carry):
        key = keys_ref[tile]
        recv = (key >> 8) & 511
        slot = ((key >> 17) << 8) | (key & 255)
        low = ends_ref[2 * tile]
        high = ends_ref[2 * tile + 1]
        hot = onehot(recv, rows)
        bias = bias_ref[...]
        pre_ref[...] = (
            dot(recv_ref[...], hot)
            + chunk_of(low, slot)
            + jnp.concatenate([bias] * (TILE // 128), axis=1)
        )

        def more(index, inner):
            pre_ref[...] += chunk_of(index, slot)
            return inner

        lax.fori_loop(low + 1, high + 1, more, 0)
        half = 0.5 * pre_ref[...]
        message = (half + half * jnp.tanh(half)).astype(BF16)
        agg_ref[...] += dot_nt(hot, message)
        return carry

    lax.fori_loop(first, last, body, 0)


def local_tiles(ends_ref, tiles, local_chunks):
    def count(tile, total):
        return total + jnp.where(ends_ref[2 * tile + 1] < local_chunks, 1, 0)

    return lax.fori_loop(0, tiles, count, 0)


def local_kernel(
    ends_ref, keys_ref, x_ref, w_ref, bias_ref, table_ref, recv_ref, agg_ref, pre_ref, bias_wide
):
    proj = dot(x_ref[...], w_ref[...])
    recv_ref[...] = jnp.transpose(proj).astype(BF16)
    bias_wide[...] = jnp.broadcast_to(bias_ref[...], bias_wide.shape)
    agg_ref[...] = jnp.zeros_like(agg_ref)
    tiles = keys_ref.shape[0]
    split = local_tiles(ends_ref, tiles, x_ref.shape[0] // CHUNK)
    edge_tiles(0, split, ends_ref, keys_ref, table_ref, recv_ref, bias_wide, pre_ref, agg_ref)


def finish_rows(agg, x, w_message, msg_gain, w_lift, attn_gain):
    high = agg.astype(BF16)
    low = (agg - high.astype(F32)).astype(BF16)
    mixed = dot(high, w_message) + dot(low, w_message)
    normed = rms_scale(mixed, msg_gain).astype(BF16)
    state = (x.astype(F32) + dot(normed, w_lift)).astype(BF16)
    return state, rms_scale(state.astype(F32), attn_gain).astype(BF16)


def remote_kernel(
    ends_ref,
    keys_ref,
    x_ref,
    bias_ref,
    recv_ref,
    agg_in_ref,
    msg_gain_ref,
    attn_gain_ref,
    sent_hbm,
    come_hbm,
    w_message_hbm,
    w_lift_hbm,
    agg_mid_ref,
    state_ref,
    top_ref,
    bottom_ref,
    table_ref,
    w_message,
    w_lift,
    agg_ref,
    pre_ref,
    bias_wide,
    sems,
):
    own = sent_hbm.shape[0]
    copies = [
        pltpu.make_async_copy(sent_hbm, table_ref.at[pl.ds(0, own)], sems.at[0]),
        pltpu.make_async_copy(come_hbm, table_ref.at[pl.ds(own, come_hbm.shape[0])], sems.at[1]),
        pltpu.make_async_copy(w_message_hbm, w_message, sems.at[2]),
        pltpu.make_async_copy(w_lift_hbm, w_lift, sems.at[3]),
    ]
    for copy in copies:
        copy.start()
    agg_ref[...] = agg_in_ref[...]
    bias_wide[...] = jnp.broadcast_to(bias_ref[...], bias_wide.shape)
    tiles = keys_ref.shape[0]
    split = local_tiles(ends_ref, tiles, x_ref.shape[0] // CHUNK)
    copies[0].wait()
    copies[1].wait()
    edge_tiles(split, tiles, ends_ref, keys_ref, table_ref, recv_ref, bias_wide, pre_ref, agg_ref)
    copies[2].wait()
    copies[3].wait()
    rows = x_ref.shape[0]
    agg_mid_ref[...] = agg_ref[pl.ds(WIN, rows - 2 * WIN), :]
    agg = jnp.concatenate([agg_ref[:WIN], agg_ref[rows - WIN :]], axis=0)
    x = jnp.concatenate([x_ref[:WIN], x_ref[rows - WIN :]], axis=0)
    state, attn_in = finish_rows(
        agg, x, w_message[...], msg_gain_ref[...], w_lift[...], attn_gain_ref[...]
    )
    state_ref[...] = state
    top_ref[...] = attn_in[:WIN]
    bottom_ref[...] = attn_in[WIN:]


def attend(q, k, v, apart, reach, scale):
    lane = lax.broadcasted_iota(jnp.int32, q.shape, 1)
    zero = jnp.zeros_like(q)
    both = jnp.concatenate([jnp.where(lane < 64, q, zero), jnp.where(lane >= 64, q, zero)], axis=0)
    score = dot_nt(both, k)
    parts = []
    rows = q.shape[0]
    for head in range(2):
        one = score[head * rows : (head + 1) * rows]
        one = jnp.where(apart <= reach[head], one, NEG)
        top = jnp.max(one, axis=-1, keepdims=True)
        parts.append(jnp.exp2((one - top) * scale).astype(BF16))
    weights = jnp.concatenate(parts, axis=0)
    wide = jnp.concatenate([v, jnp.ones((v.shape[0], 128), BF16)], axis=1)
    mixed = dot(weights, wide)
    out = mixed[:, :128] / mixed[:, 128:]
    return jnp.where(lane < 64, out[:rows], out[rows:]).astype(BF16)


def distance(rows, keys):
    q_at = lax.broadcasted_iota(jnp.int32, (rows, keys), 0) + WIN
    k_at = lax.broadcasted_iota(jnp.int32, (rows, keys), 1)
    return jnp.abs(q_at - k_at), k_at


LOG2E = 1.4426950408889634


def inner_kernel(
    reach_ref,
    agg_ref,
    x_ref,
    state_tb_ref,
    top_ref,
    bottom_ref,
    msg_gain_ref,
    attn_gain_ref,
    w_message_hbm,
    w_lift_hbm,
    w_q_hbm,
    w_k_hbm,
    w_v_hbm,
    w_out_hbm,
    q_ref,
    k_ref,
    v_ref,
    res_ref,
    w_message,
    w_lift,
    w_q,
    w_k,
    w_v,
    w_out,
    attn_ref,
    q_mid,
    mix_ref,
    apart_ref,
    sems,
):
    pairs = [
        (w_message_hbm, w_message),
        (w_lift_hbm, w_lift),
        (w_q_hbm, w_q),
        (w_k_hbm, w_k),
        (w_v_hbm, w_v),
        (w_out_hbm, w_out),
    ]
    copies = [pltpu.make_async_copy(a, b, sems.at[i]) for i, (a, b) in enumerate(pairs)]
    for copy in copies:
        copy.start()
    rows = x_ref.shape[0]
    mid = rows - 2 * WIN
    copies[0].wait()
    copies[1].wait()
    state, attn_in = finish_rows(
        agg_ref[...],
        x_ref[pl.ds(WIN, mid), :],
        w_message[...],
        msg_gain_ref[...],
        w_lift[...],
        attn_gain_ref[...],
    )
    attn_ref[pl.ds(0, WIN), :] = top_ref[...]
    attn_ref[pl.ds(rows - WIN, WIN), :] = bottom_ref[...]
    attn_ref[pl.ds(WIN, mid), :] = attn_in
    copies[2].wait()
    q = dot(attn_ref[...], w_q[...]).astype(BF16)
    q_ref[pl.ds(0, WIN), :] = q[:WIN]
    q_ref[pl.ds(WIN, WIN), :] = q[rows - WIN :]
    q_mid[...] = q[WIN : rows - WIN]
    copies[3].wait()
    k_ref[...] = dot(attn_ref[...], w_k[...]).astype(BF16)
    copies[4].wait()
    v_ref[...] = dot(attn_ref[...], w_v[...]).astype(BF16)
    apart_ref[...] = distance(WIN, 3 * WIN)[0]

    def body(pair, carry):
        lanes = pl.ds(pl.multiple_of(pair * 128, 128), 128)
        reach = (reach_ref[2 * pair], reach_ref[2 * pair + 1])
        for block in range(2):
            keys = pl.ds(block * WIN, 3 * WIN)
            mix_ref[pl.ds(block * WIN, WIN), lanes] = attend(
                q_mid[pl.ds(block * WIN, WIN), lanes],
                k_ref[keys, lanes],
                v_ref[keys, lanes],
                apart_ref[...],
                reach,
                0.125 * LOG2E,
            )
        return carry

    lax.fori_loop(0, q_ref.shape[1] // 128, body, 0)
    copies[5].wait()
    res_ref[...] = (state.astype(F32) + dot(mix_ref[...], w_out[...])).astype(BF16)


def outer_kernel(
    reach_ref,
    q_ref,
    left_ref,
    right_ref,
    k_ref,
    v_ref,
    state_ref,
    w_k_hbm,
    w_v_hbm,
    w_out_hbm,
    res_hbm,
    out_hbm,
    w_k,
    w_v,
    w_out,
    keys_ref,
    values_ref,
    apart_ref,
    mix_ref,
    fin_ref,
    sems,
):
    rows = k_ref.shape[0]
    pairs = [
        (w_k_hbm, w_k),
        (w_v_hbm, w_v),
        (w_out_hbm, w_out),
        (res_hbm, out_hbm.at[pl.ds(WIN, rows - 2 * WIN)]),
    ]
    copies = [pltpu.make_async_copy(a, b, sems.at[i]) for i, (a, b) in enumerate(pairs)]
    for copy in copies:
        copy.start()
    halo = jnp.concatenate([left_ref[...], right_ref[...]], axis=0)
    two = 2 * WIN
    keys_ref[0, pl.ds(WIN, two), :] = k_ref[pl.ds(0, two), :]
    keys_ref[1, pl.ds(0, two), :] = k_ref[pl.ds(rows - two, two), :]
    values_ref[0, pl.ds(WIN, two), :] = v_ref[pl.ds(0, two), :]
    values_ref[1, pl.ds(0, two), :] = v_ref[pl.ds(rows - two, two), :]
    apart, k_at = distance(WIN, 3 * WIN)
    heads = reach_ref.shape[0] - 2
    apart_ref[0] = jnp.where((k_at < WIN) & (reach_ref[heads] != 0), BIG, apart)
    apart_ref[1] = jnp.where((k_at >= two) & (reach_ref[heads + 1] != 0), BIG, apart)
    copies[0].wait()
    k_halo = dot(halo, w_k[...]).astype(BF16)
    keys_ref[0, pl.ds(0, WIN), :] = k_halo[:WIN]
    keys_ref[1, pl.ds(two, WIN), :] = k_halo[WIN:]
    copies[1].wait()
    v_halo = dot(halo, w_v[...]).astype(BF16)
    values_ref[0, pl.ds(0, WIN), :] = v_halo[:WIN]
    values_ref[1, pl.ds(two, WIN), :] = v_halo[WIN:]

    def body(pair, carry):
        lanes = pl.ds(pl.multiple_of(pair * 128, 128), 128)
        reach = (reach_ref[2 * pair], reach_ref[2 * pair + 1])
        for block in range(2):
            mix_ref[pl.ds(block * WIN, WIN), lanes] = attend(
                q_ref[pl.ds(block * WIN, WIN), lanes],
                keys_ref[block, :, lanes],
                values_ref[block, :, lanes],
                apart_ref[block],
                reach,
                0.125 * LOG2E,
            )
        return carry

    lax.fori_loop(0, q_ref.shape[1] // 128, body, 0)
    copies[2].wait()
    fin_ref[...] = (state_ref[...].astype(F32) + dot(mix_ref[...], w_out[...])).astype(BF16)
    ends = [
        pltpu.make_async_copy(fin_ref.at[pl.ds(0, WIN)], out_hbm.at[pl.ds(0, WIN)], sems.at[4]),
        pltpu.make_async_copy(
            fin_ref.at[pl.ds(WIN, WIN)], out_hbm.at[pl.ds(rows - WIN, WIN)], sems.at[5]
        ),
    ]
    for copy in ends:
        copy.start()
    copies[3].wait()
    for copy in ends:
        copy.wait()


def call(kernel, name, out_shape, in_specs, out_specs, scratch, flops, moved):
    return pl.pallas_call(
        kernel,
        name=name,
        out_shape=out_shape,
        in_specs=in_specs,
        out_specs=out_specs,
        scratch_shapes=scratch,
        compiler_params=pltpu.CompilerParams(vmem_limit_bytes=LIMIT),
        cost_estimate=pl.CostEstimate(flops=flops, bytes_accessed=moved, transcendentals=0),
    )


def local(
    node_state,
    edge_recv,
    edge_send,
    halo_rows,
    window_reach,
    w_recv,
    w_send,
    edge_bias,
    w_message,
    msg_gain,
    w_lift,
    attn_gain,
    w_qkv,
    w_out,
):
    shape = jax.ShapeDtypeStruct
    rows, width = node_state.shape
    hidden = w_recv.shape[1]
    peers, halo = halo_rows.shape[1:]
    edges = edge_recv.shape[0]
    heads = w_qkv.shape[1]
    size = w_qkv.shape[2] // 3
    tiles = edges // TILE
    dma = pltpu.SemaphoreType.DMA
    mega = 1 << 20

    table, outgoing = call(
        send_kernel,
        "send",
        (shape((rows // 128, hidden, 128), BF16), shape((peers, hidden, halo), BF16)),
        [VMEM] * 3,
        (VMEM, VMEM),
        [],
        4 << 30,
        4 * mega,
    )(node_state, w_send, halo_rows.reshape(peers, halo))
    incoming = lax.all_to_all(outgoing, "node", split_axis=0, concat_axis=0, tiled=True)

    keys = lax.sort(((edge_send >> 8) << 17) | (edge_recv << 8) | (edge_send & 255))
    tiled = keys.reshape(tiles, TILE)
    ends = (jnp.stack([tiled[:, 0], tiled[:, -1]], axis=1) >> 17).reshape(-1)
    keys = keys.reshape(tiles, 1, TILE)
    bias = edge_bias.reshape(hidden, 1)
    recv, agg = call(
        local_kernel,
        "local_edges",
        (shape((hidden, rows), BF16), shape((rows, hidden), F32)),
        [SMEM] + [VMEM] * 5,
        (VMEM, VMEM),
        [pltpu.VMEM((hidden, TILE), F32), pltpu.VMEM((hidden, 128), F32)],
        10 << 30,
        4 * mega,
    )(ends, keys, node_state, w_recv, bias, table)
    split_qkv = w_qkv.reshape(width, heads, 3, size)
    w_q, w_k, w_v = (split_qkv[:, :, i].reshape(width, heads * size) for i in range(3))

    gain_m = msg_gain.reshape(1, hidden)
    gain_a = attn_gain.reshape(1, width)
    agg_mid, state_tb, top, bottom = call(
        remote_kernel,
        "remote_edges",
        (
            shape((rows - 2 * WIN, hidden), F32),
            shape((2 * WIN, width), BF16),
            shape((WIN, width), BF16),
            shape((WIN, width), BF16),
        ),
        [SMEM] + [VMEM] * 7 + [ANY] * 4,
        (VMEM,) * 4,
        [
            pltpu.VMEM((rows // 128 + peers, hidden, 128), BF16),
            pltpu.VMEM((hidden, hidden), BF16),
            pltpu.VMEM((hidden, width), BF16),
            pltpu.VMEM((rows, hidden), F32),
            pltpu.VMEM((hidden, TILE), F32),
            pltpu.VMEM((hidden, 128), F32),
            dma((4,)),
        ],
        10 << 30,
        4 * mega,
    )(ends, keys, node_state, bias, recv, agg, gain_m, gain_a, table, incoming, w_message, w_lift)

    nodes = lax.axis_size("node")
    me = lax.axis_index("node")
    left = lax.ppermute(bottom, "node", [(i, (i + 1) % nodes) for i in range(nodes)])
    right = lax.ppermute(top, "node", [(i, (i - 1) % nodes) for i in range(nodes)])
    reach = jnp.concatenate(
        [window_reach, jnp.stack([me == 0, me == nodes - 1]).astype(jnp.int32)]
    )

    q_tb, k, v, res_mid = call(
        inner_kernel,
        "inner",
        (
            shape((2 * WIN, width), BF16),
            shape((rows, width), BF16),
            shape((rows, width), BF16),
            shape((rows - 2 * WIN, width), BF16),
        ),
        [SMEM] + [VMEM] * 7 + [ANY] * 6,
        (VMEM,) * 4,
        [
            pltpu.VMEM((hidden, hidden), BF16),
            pltpu.VMEM((hidden, width), BF16),
            pltpu.VMEM((width, width), BF16),
            pltpu.VMEM((width, width), BF16),
            pltpu.VMEM((width, width), BF16),
            pltpu.VMEM((width, width), BF16),
            pltpu.VMEM((rows, width), BF16),
            pltpu.VMEM((rows - 2 * WIN, width), BF16),
            pltpu.VMEM((rows - 2 * WIN, width), BF16),
            pltpu.VMEM((WIN, 3 * WIN), jnp.int32),
            dma((6,)),
        ],
        10 << 30,
        12 * mega,
    )(
        reach,
        agg_mid,
        node_state,
        state_tb,
        top,
        bottom,
        gain_m,
        gain_a,
        w_message,
        w_lift,
        w_q,
        w_k,
        w_v,
        w_out,
    )

    return call(
        outer_kernel,
        "outer",
        shape((rows, width), BF16),
        [SMEM] + [VMEM] * 6 + [ANY] * 4,
        ANY,
        [
            pltpu.VMEM((width, width), BF16),
            pltpu.VMEM((width, width), BF16),
            pltpu.VMEM((width, width), BF16),
            pltpu.VMEM((2, 3 * WIN, width), BF16),
            pltpu.VMEM((2, 3 * WIN, width), BF16),
            pltpu.VMEM((2, WIN, 3 * WIN), jnp.int32),
            pltpu.VMEM((2 * WIN, width), BF16),
            pltpu.VMEM((2 * WIN, width), BF16),
            dma((6,)),
        ],
        6 << 30,
        12 * mega,
    )(reach, q_tb, left, right, k, v, state_tb, w_k, w_v, w_out, res_mid)


def solution(mesh):
    split = ("dp", "node")
    in_specs = (P(split, None), P(split), P(split), P(split, None, None)) + (P(),) * 10
    return jax.shard_map(
        local, mesh=mesh, in_specs=in_specs, out_specs=P(split, None), check_vma=False
    )
```

time: 411 us -> 94.7 us (0.23)
  matrix products: 113 us -> 0 us
  local copies, waits for them, and re-layouts: 117 us -> 34.5 us
  other arithmetic: 80.6 us -> 5.95 us
  waiting for transfers between devices: 55.2 us -> 0.01 us
  Pallas kernels: 0 us -> 40.3 us
  blocking collectives: 19.8 us -> 0 us
  loops' own time: 9.71 us -> 0 us
    dot_general x37 -> x0, matrix products: 106 us -> none  [the longest x16 48.2 us: attend(): jnp.einsum('hqk,khd->qhd', weights, values, preferred_element_type=jnp.fl...]
    reshape x1 -> x0, other arithmetic: 46.5 us -> none  [local(): head_out = blocks.reshape(total, per_dev, width)]
    gather x3 -> x0, local copies, waits for them, and re-layouts: 46 us -> none  [the longest x1 19.6 us: local(): jnp.take(table, edge_send, axis=0).astype(jnp.float32)]
    all_to_all x1 -> x0, waiting for transfers between devices: 43.1 us -> none  [local(): owned = lax.all_to_all(qkv, 'node', split_axis=1, concat_axis=0, tiled=True)]
    pallas_call x0 -> x5, Pallas kernels: none -> 40.3 us  [the longest x1 11.6 us: local(): call(inner_kernel, 'inner', (shape((2 * WIN, width), BF16), shape((rows,...]
    reduce_sum x16 -> x0, other arithmetic: 24 us -> none  [attend(): jnp.sum(expo, axis=-1, keepdims=True)]
    all_to_all x1 -> x0, blocking collectives: 19.8 us -> none  [local(): lax.all_to_all(head_out, 'node', split_axis=0, concat_axis=1, tiled=True)]
    while x32 -> x0, local copies, waits for them, and re-layouts: 18.5 us -> none
  transfers between devices with their start and end apart: 2 -> 3, of which waited for: 2 -> 0; matrix products, arithmetic and copies ran while one was open for 5% -> 26% of each run, Pallas kernels for 0% -> 21%
where the time goes in v1:
time: 94.7 us; the launch traced here: 93.8 us
  Pallas kernels  40.3 us (43%)
  local copies, waits for them, and re-layouts  34.5 us (36%)
  starting transfers between devices  12.7 us (13%)
  other arithmetic  5.95 us (6%)
    unnamed x52, local copies, waits for them, and re-layouts  16.2 us
    another operation x3, local copies, waits for them, and re-layouts, local(): split_qkv[:, :, i].reshape(width, heads * size)  11.9 us
    pallas_call x1, Pallas kernels, local(): call(inner_kernel, 'inner', (shape((2 * WIN, width), BF16), shape((rows,...  11.6 us
    pallas_call x1, Pallas kernels, local(): call(outer_kernel, 'outer', shape((rows, width), BF16), [SMEM] + [VMEM] *...  9.35 us
    pallas_call x1, Pallas kernels, local(): call(remote_kernel, 'remote_edges', (shape((rows - 2 * WIN, hidden), F32)...  9.17 us
    pallas_call x1, Pallas kernels, local(): call(local_kernel, 'local_edges', (shape((hidden, rows), BF16), shape((ro...  8.25 us
    all_to_all x1, starting transfers between devices, local(): lax.all_to_all(outgoing, 'node', split_axis=0, concat_axis=0, tiled=True)  7.17 us
    slice x1, local copies, waits for them, and re-layouts, local(): split_qkv[:, :, i].reshape(width, heads * size)  5.8 us
  transfers between devices with their start and end apart: 3, of which 0 were waited for; matrix products, arithmetic and copies ran while one was open for 26% of the time, Pallas kernels for 21%

profile of v1, /device:TPU:224, one launch (start us, length us, event | category | flops | bytes accessed | tf_op | source)
XLA Modules:
  0.0 93.8 jit_solution(14729420377305911821)
XLA Ops:
  0.0 0.0 copy-start.4
  0.0 1.2 %copy-done.4 = bf16[1024,512]{1,0:T(8,128)(2,1)S(1)} copy-done((bf16[1024,512]{1,0:T(8,128)(2,1)S(1)}, bf16[1024,512]{1,0:T(8,128)(2,1)}, u32[]{:S(2)}) %copy-start.4) | copy-done | bytes 1048600
  1.2 0.0 copy-start.6
  1.2 1.2 %copy-done.6 = bf16[512,1024]{1,0:T(8,128)(2,1)S(1)} copy-done((bf16[512,1024]{1,0:T(8,128)(2,1)S(1)}, bf16[512,1024]{1,0:T(8,128)(2,1)}, u32[]{:S(2)}) %copy-start.6) | copy-done | bytes 1048600
  2.5 0.0 copy-start.12
  2.5 0.7 copy-done.12
  3.1 1.9 %send.1 = (bf16[4,512,128]{2,1,0:T(8,128)(2,1)S(1)}, bf16[16,512,128]{2,1,0:T(8,128)(2,1)S(1)}) custom-call(bf16[512,1024]{1,0:T(8,128)(2,1)S(1)} %copy-done.6, bf16[1024,512]{1,0:T(8,128)(2,1)S(1)} %copy-done.4, s32[16,128]{1,0:T(8,128)S(1)} %bitcast.13), custom_call_target="tpu_custom_call" | custom-call | flops 4294967296 | bytes 4194304 | tf_op jit(solution)/shard_map/send/pallas_call | solution.py:411
  5.1 0.0 copy-start.2
  5.1 1.3 %copy-done.2 = bf16[16,512,128]{2,1,0:T(8,128)(2,1)} copy-done((bf16[16,512,128]{2,1,0:T(8,128)(2,1)}, bf16[16,512,128]{2,1,0:T(8,128)(2,1)S(1)}, u32[]{:S(2)}) %copy-start.2) | copy-done | bytes 2097176
  6.4 0.0 copy-start.15
  6.4 0.8 copy-done.15
  7.2 0.0 copy-start.22
  7.2 0.0 copy-start.23
  7.2 0.0 copy-start.24
  7.2 7.2 %all-to-all-start = ((bf16[16,512,128]{2,1,0:T(8,128)(2,1)}), bf16[16,512,128]{2,1,0:T(8,128)(2,1)S(1)}, u32[]{:S(2)}, u32[]{:S(2)}) async-start(bf16[16,512,128]{2,1,0:T(8,128)(2,1)} %copy-done.2), calls=%async_computation | async-start | bytes 4194304 | tf_op jit(solution)/shard_map/all_to_all | solution.py:421
  14.4 0.0 copy-done.22
  14.4 0.0 copy-done.23
  14.5 5.8 %sort.14 = (s32[4096]{0:T(1024)S(1)}, s32[4096]{0:T(1024)}) sort(s32[4096]{0:T(1024)S(1)} %and_or_fusion, s32[4096]{0:T(1024)S(1)} %iota.3), dimensions={0}, to_apply=%region_0.0 | sort | flops 49152 | bytes 65536 | tf_op jit(solution)/shard_map/sort | solution.py:423
  20.2 0.1 fusion.1
  20.3 0.1 copy.40
  20.4 0.1 copy.41
  20.5 0.1 copy.42
  20.6 0.1 shift_right_arithmetic.16.ends_ref
  20.7 0.0 copy-done.24
  20.7 0.1 copy.44.bias_ref
  20.8 5.8 %fusion = (bf16[1024,16,1,64]{0,3,2,1:T(8,128)(2,1)}, bf16[1024,16,1,64]{0,3,2,1:T(8,128)(2,1)}, bf16[1024,16,1,64]{0,3,2,1:T(8,128)(2,1)}) fusion(bf16[1024,16,3,64]{0,3,2,1:T(8,128)(2,1)} %bitcast.21), kind=kLoop, calls=%fused_computation.4 | loop fusion | bytes 12582912 | tf_op jit(solution)/shard_map/slice | solution.py:439
  26.6 3.9 %copy.46.w_k_hbm = bf16[1024,1024]{1,0:T(8,128)(2,1)} copy(bf16[1024,1024]{0,1:T(8,128)(2,1)} %bitcast.20) | data formatting | bytes 4194304 | tf_op jit(solution)/shard_map/reshape;squeeze | solution.py:439
  30.6 4.0 %copy.47.w_v_hbm = bf16[1024,1024]{1,0:T(8,128)(2,1)} copy(bf16[1024,1024]{0,1:T(8,128)(2,1)} %bitcast.19) | data formatting | bytes 4194304 | tf_op jit(solution)/shard_map/reshape;squeeze | solution.py:439
  34.5 0.0 copy-start.25
  34.5 0.0 copy-start.5
  34.5 4.0 %copy.45.w_q_hbm = bf16[1024,1024]{1,0:T(8,128)(2,1)} copy(bf16[1024,1024]{0,1:T(8,128)(2,1)} %bitcast.18) | data formatting | bytes 4194304 | tf_op jit(solution)/shard_map/reshape;squeeze | solution.py:439
  38.6 0.1 add_convert_fusion
  38.6 0.0 copy-done.25
  38.6 0.1 pad_add_fusion.reach_ref
  38.7 0.0 copy-done.5
  38.7 0.0 copy-start.7
  38.7 1.2 %copy-done.7 = bf16[512,1024]{1,0:T(8,128)(2,1)S(1)} copy-done((bf16[512,1024]{1,0:T(8,128)(2,1)S(1)}, bf16[512,1024]{1,0:T(8,128)(2,1)}, u32[]{:S(2)}) %copy-start.7) | copy-done | bytes 1048600
  39.9 0.0 copy-start.16
  39.9 1.0 %copy-done.16 = bf16[4,512,128]{2,1,0:T(8,128)(2,1)S(1)} copy-done((bf16[4,512,128]{2,1,0:T(8,128)(2,1)S(1)}, bf16[4,512,128]{2,1,0:T(8,128)(2,1)}, u32[]{:S(2)}) %copy-start.16) | copy-done | bytes 524312
  41.0 8.3 %local_edges.1 = (bf16[512,512]{1,0:T(8,128)(2,1)S(1)}, f32[512,512]{1,0:T(8,128)S(1)}) custom-call(s32[32]{0:T(128)S(1)} %shift_right_arithmetic.16.ends_ref, s32[16,1,256]{2,1,0:T(1,128)S(1)} %bitcast.11, bf16[512,1024]{1,0:T(8,128)(2,1)S(1)} %copy-done.7, bf16[1024,512]{1,0:T(8,128)(2,1)S(1)} %copy-done.5, f32[512,1]{1,0:T(8,128)S(1)} %copy.44.bias_ref, ...), custom_call_target="tpu_custom_call" | custom-call | flops 10737418240 | bytes 4194304 | tf_op jit(solution)/shard_map/local_edges/pallas_call | solution.py:428
  49.3 0.0 copy-start.18
  49.3 1.0 %copy-done.18 = f32[512,512]{1,0:T(8,128)} copy-done((f32[512,512]{1,0:T(8,128)}, f32[512,512]{1,0:T(8,128)S(1)}, u32[]{:S(2)}) %copy-start.18) | copy-done | bytes 1048600
  50.2 0.8 copy-done.20
  51.0 0.0 all-to-all-done.come_hbm
  51.0 0.0 copy-done.13
  51.1 0.0 copy-done.14
  51.1 0.0 copy-start.8
  51.1 1.2 %copy-done.8 = bf16[512,1024]{1,0:T(8,128)(2,1)S(1)} copy-done((bf16[512,1024]{1,0:T(8,128)(2,1)S(1)}, bf16[512,1024]{1,0:T(8,128)(2,1)}, u32[]{:S(2)}) %copy-start.8) | copy-done | bytes 1048600
  52.3 1.2 %copy-done.10 = bf16[512,1024]{1,0:T(8,128)(2,1)S(1)} copy-done((bf16[512,1024]{1,0:T(8,128)(2,1)S(1)}, bf16[512,1024]{1,0:T(8,128)(2,1)}, u32[]{:S(2)}) %copy-start.10) | copy-done | bytes 1048600
  53.5 1.0 %copy-done.11 = bf16[512,512]{1,0:T(8,128)(2,1)S(1)} copy-done((bf16[512,512]{1,0:T(8,128)(2,1)S(1)}, bf16[512,512]{1,0:T(8,128)(2,1)}, u32[]{:S(2)}) %copy-start.11) | copy-done | bytes 524312
  54.6 1.0 %copy-done.17 = bf16[4,512,128]{2,1,0:T(8,128)(2,1)S(1)} copy-done((bf16[4,512,128]{2,1,0:T(8,128)(2,1)S(1)}, bf16[4,512,128]{2,1,0:T(8,128)(2,1)}, u32[]{:S(2)}) %copy-start.17) | copy-done | bytes 524312
  55.6 1.2 %copy-done.19 = f32[512,512]{1,0:T(8,128)S(1)} copy-done((f32[512,512]{1,0:T(8,128)S(1)}, f32[512,512]{1,0:T(8,128)}, u32[]{:S(2)}) %copy-start.19) | copy-done | bytes 1048600
  56.8 1.0 %copy-done.21 = bf16[512,512]{1,0:T(8,128)(2,1)S(1)} copy-done((bf16[512,512]{1,0:T(8,128)(2,1)S(1)}, bf16[512,512]{1,0:T(8,128)(2,1)}, u32[]{:S(2)}) %copy-start.21) | copy-done | bytes 524312
  57.9 9.2 %remote_edges.1 = (f32[256,512]{1,0:T(8,128)S(1)}, bf16[256,1024]{1,0:T(8,128)(2,1)S(1)}, bf16[128,1024]{1,0:T(8,128)(2,1)S(1)}, bf16[128,1024]{1,0:T(8,128)(2,1)S(1)}) custom-call(s32[32]{0:T(128)S(1)} %shift_right_arithmetic.16.ends_ref, s32[16,1,256]{2,1,0:T(1,128)S(1)} %bitcast.12, bf16[512,1024]{1,0:T(8,128)(2,1)S(1)} %copy-done.8, ...), custom_call_target="tpu_custom_call" | custom-call | flops 10737418240 | bytes 4194304 | tf_op jit(solution)/shard_map/remote_edges/pallas_call | solution.py:443
  67.0 2.0 %collective-permute-start = (bf16[128,1024]{1,0:T(8,128)(2,1)S(1)}, bf16[128,1024]{1,0:T(8,128)(2,1)S(1)}, u32[]{:S(2)}, u32[]{:S(2)}) collective-permute-start(bf16[128,1024]{1,0:T(8,128)(2,1)S(1)} %get-tuple-element.27.bottom_ref), channel_id=1, source_target_pairs={{0,1},{1,2},{2,3},{3,4},{4,5},{5,6},{6,7},{7,8},{8,9},{9,10},{10,1... | collective-permute-start | bytes 786440 | tf_op jit(solution)/shard_map/ppermute | solution.py:469
  69.0 3.6 %collective-permute-start.1 = (bf16[128,1024]{1,0:T(8,128)(2,1)S(1)}, bf16[128,1024]{1,0:T(8,128)(2,1)S(1)}, u32[]{:S(2)}, u32[]{:S(2)}) collective-permute-start(bf16[128,1024]{1,0:T(8,128)(2,1)S(1)} %get-tuple-element.26.top_ref), channel_id=1, source_target_pairs={{0,15},{1,0},{2,1},{3,2},{4,3},{5,4},{6,5},{7,6},{8,7},{9,8},{10,9... | collective-permute-start | bytes 786440 | tf_op jit(solution)/shard_map/ppermute | solution.py:470
  72.6 0.0 copy-done.3
  72.6 0.0 copy-done.9
  72.6 11.6 %inner.1 = (bf16[256,1024]{1,0:T(8,128)(2,1)S(1)}, bf16[512,1024]{1,0:T(8,128)(2,1)S(1)}, bf16[512,1024]{1,0:T(8,128)(2,1)S(1)}, bf16[256,1024]{1,0:T(8,128)(2,1)S(1)}) custom-call(s32[18]{0:T(128)S(1)} %pad_add_fusion.reach_ref, f32[256,512]{1,0:T(8,128)S(1)} %get-tuple-element.24.agg_ref, bf16[512,1024]{1,0:T(8,128)(2,1)S(1)} %copy-done.9, ...), custom_call_target="tpu_custom_call" | custom-call | flops 10737418240 | bytes 12582912 | tf_op jit(solution)/shard_map/inner/pallas_call | solution.py:475
  84.3 0.0 collective-permute-done.left_ref
  84.3 0.0 collective-permute-done.1.right_ref
  84.3 0.0 copy-done
  84.3 0.0 copy-done.1
  84.3 9.3 %outer.1 = bf16[512,1024]{1,0:T(8,128)(2,1)} custom-call(s32[18]{0:T(128)S(1)} %pad_add_fusion.reach_ref, bf16[256,1024]{1,0:T(8,128)(2,1)S(1)} %get-tuple-element.28.q_ref, bf16[128,1024]{1,0:T(8,128)(2,1)S(1)} %collective-permute-done.left_ref, bf16[128,1024]{1,0:T(8,128)(2,1)S(1)} %collective-permute-done.1.right_ref, ...), custom_call_target="tpu_custom_call" | custom-call | flops 6442450944 | bytes 12582912 | tf_op jit(solution)/shard_map/outer/pallas_call | solution.py:518
  (16 shorter events, 0.0 us)
Async XLA Ops:
  0.0 1.2 %copy-start.4 = (bf16[1024,512]{1,0:T(8,128)(2,1)S(1)}, bf16[1024,512]{1,0:T(8,128)(2,1)}, u32[]{:S(2)}) copy-start(bf16[1024,512]{1,0:T(8,128)(2,1)} %w_ref.2) | copy-start | bytes 3145732
  1.2 1.2 %copy-start.6 = (bf16[512,1024]{1,0:T(8,128)(2,1)S(1)}, bf16[512,1024]{1,0:T(8,128)(2,1)}, u32[]{:S(2)}) copy-start(bf16[512,1024]{1,0:T(8,128)(2,1)} %x_ref.7) | copy-start | bytes 3145732
  2.5 0.7 copy-start.12
  5.1 1.3 %copy-start.2 = (bf16[16,512,128]{2,1,0:T(8,128)(2,1)}, bf16[16,512,128]{2,1,0:T(8,128)(2,1)S(1)}, u32[]{:S(2)}) copy-start(bf16[16,512,128]{2,1,0:T(8,128)(2,1)S(1)} %get-tuple-element.23) | copy-start | bytes 6291460
  6.4 0.8 copy-start.15
  7.2 7.2 %copy-start.22 = (s32[4096]{0:T(1024)S(1)}, s32[4096]{0:T(1024)}, u32[]{:S(2)}) copy-start(s32[4096]{0:T(1024)} %param.16) | copy-start | bytes 49156
  7.2 7.2 %copy-start.23 = (s32[4096]{0:T(1024)S(1)}, s32[4096]{0:T(1024)}, u32[]{:S(2)}) copy-start(s32[4096]{0:T(1024)} %param.15) | copy-start | bytes 49156
  7.2 13.4 %copy-start.24 = (f32[512]{0:T(512)S(1)}, f32[512]{0:T(512)}, u32[]{:S(2)}) copy-start(f32[512]{0:T(512)} %param.21) | copy-start | bytes 6148
  7.2 43.8 %all-to-all-start = ((bf16[16,512,128]{2,1,0:T(8,128)(2,1)}), bf16[16,512,128]{2,1,0:T(8,128)(2,1)S(1)}, u32[]{:S(2)}, u32[]{:S(2)}) async-start(bf16[16,512,128]{2,1,0:T(8,128)(2,1)} %copy-done.2), calls=%async_computation | async-start | bytes 4194304 | tf_op jit(solution)/shard_map/all_to_all | solution.py:421
  34.5 4.1 %copy-start.25 = (s32[16]{0:T(128)S(1)}, s32[16]{0:T(128)}, u32[]{:S(2)}) copy-start(s32[16]{0:T(128)} %param.18) | copy-start | bytes 196
  34.5 4.2 %copy-start.5 = (bf16[1024,512]{1,0:T(8,128)(2,1)S(1)}, bf16[1024,512]{1,0:T(8,128)(2,1)}, u32[]{:S(2)}) copy-start(bf16[1024,512]{1,0:T(8,128)(2,1)} %w_ref.3) | copy-start | bytes 3145732
  38.7 1.2 %copy-start.7 = (bf16[512,1024]{1,0:T(8,128)(2,1)S(1)}, bf16[512,1024]{1,0:T(8,128)(2,1)}, u32[]{:S(2)}) copy-start(bf16[512,1024]{1,0:T(8,128)(2,1)} %x_ref.7) | copy-start | bytes 3145732
  39.9 1.0 %copy-start.16 = (bf16[4,512,128]{2,1,0:T(8,128)(2,1)S(1)}, bf16[4,512,128]{2,1,0:T(8,128)(2,1)}, u32[]{:S(2)}) copy-start(bf16[4,512,128]{2,1,0:T(8,128)(2,1)} %copy-done.15) | copy-start | bytes 1572868
  41.0 10.1 %copy-start.13 = (f32[1024]{0:T(1024)S(1)}, f32[1024]{0:T(1024)}, u32[]{:S(2)}) copy-start(f32[1024]{0:T(1024)} %param.25) | copy-start | bytes 12292
  41.0 10.1 %copy-start.14 = (f32[512]{0:T(512)S(1)}, f32[512]{0:T(512)}, u32[]{:S(2)}) copy-start(f32[512]{0:T(512)} %param.23) | copy-start | bytes 6148
  49.3 1.0 %copy-start.18 = (f32[512,512]{1,0:T(8,128)}, f32[512,512]{1,0:T(8,128)S(1)}, u32[]{:S(2)}) copy-start(f32[512,512]{1,0:T(8,128)S(1)} %get-tuple-element.22.agg_in_ref) | copy-start | bytes 3145732
  50.2 0.8 copy-start.20
  51.1 1.2 %copy-start.8 = (bf16[512,1024]{1,0:T(8,128)(2,1)S(1)}, bf16[512,1024]{1,0:T(8,128)(2,1)}, u32[]{:S(2)}) copy-start(bf16[512,1024]{1,0:T(8,128)(2,1)} %x_ref.7) | copy-start | bytes 3145732
  52.3 1.2 %copy-start.10 = (bf16[512,1024]{1,0:T(8,128)(2,1)S(1)}, bf16[512,1024]{1,0:T(8,128)(2,1)}, u32[]{:S(2)}) copy-start(bf16[512,1024]{1,0:T(8,128)(2,1)} %w_lift_hbm.3) | copy-start | bytes 3145732
  53.5 1.0 %copy-start.11 = (bf16[512,512]{1,0:T(8,128)(2,1)S(1)}, bf16[512,512]{1,0:T(8,128)(2,1)}, u32[]{:S(2)}) copy-start(bf16[512,512]{1,0:T(8,128)(2,1)} %w_message_hbm.3) | copy-start | bytes 1572868
  54.6 1.0 %copy-start.17 = (bf16[4,512,128]{2,1,0:T(8,128)(2,1)S(1)}, bf16[4,512,128]{2,1,0:T(8,128)(2,1)}, u32[]{:S(2)}) copy-start(bf16[4,512,128]{2,1,0:T(8,128)(2,1)} %copy-done.15) | copy-start | bytes 1572868
  55.6 1.2 %copy-start.19 = (f32[512,512]{1,0:T(8,128)S(1)}, f32[512,512]{1,0:T(8,128)}, u32[]{:S(2)}) copy-start(f32[512,512]{1,0:T(8,128)} %copy-done.18) | copy-start | bytes 3145732
  56.8 1.0 %copy-start.21 = (bf16[512,512]{1,0:T(8,128)(2,1)S(1)}, bf16[512,512]{1,0:T(8,128)(2,1)}, u32[]{:S(2)}) copy-start(bf16[512,512]{1,0:T(8,128)(2,1)} %copy-done.20) | copy-start | bytes 1572868
  57.9 14.8 %copy-start.3 = (bf16[1024,1024]{1,0:T(8,128)(2,1)S(1)}, bf16[1024,1024]{1,0:T(8,128)(2,1)}, u32[]{:S(2)}) copy-start(bf16[1024,1024]{1,0:T(8,128)(2,1)} %copy.45.w_q_hbm) | copy-start | bytes 6291460
  57.9 14.8 %copy-start.9 = (bf16[512,1024]{1,0:T(8,128)(2,1)S(1)}, bf16[512,1024]{1,0:T(8,128)(2,1)}, u32[]{:S(2)}) copy-start(bf16[512,1024]{1,0:T(8,128)(2,1)} %x_ref.7) | copy-start | bytes 3145732
  67.0 17.2 %collective-permute-start = (bf16[128,1024]{1,0:T(8,128)(2,1)S(1)}, bf16[128,1024]{1,0:T(8,128)(2,1)S(1)}, u32[]{:S(2)}, u32[]{:S(2)}) collective-permute-start(bf16[128,1024]{1,0:T(8,128)(2,1)S(1)} %get-tuple-element.27.bottom_ref), channel_id=1, source_target_pairs={{0,1},{1,2},{2,3},{3,4},{4,5},{5,6},{6,7},{7,8},{8,9},{9,10},{10,1... | collective-permute-start | bytes 786440 | tf_op jit(solution)/shard_map/ppermute | solution.py:469
  69.0 15.2 %collective-permute-start.1 = (bf16[128,1024]{1,0:T(8,128)(2,1)S(1)}, bf16[128,1024]{1,0:T(8,128)(2,1)S(1)}, u32[]{:S(2)}, u32[]{:S(2)}) collective-permute-start(bf16[128,1024]{1,0:T(8,128)(2,1)S(1)} %get-tuple-element.26.top_ref), channel_id=1, source_target_pairs={{0,15},{1,0},{2,1},{3,2},{4,3},{5,4},{6,5},{7,6},{8,7},{9,8},{10,9... | collective-permute-start | bytes 786440 | tf_op jit(solution)/shard_map/ppermute | solution.py:470
  72.6 11.7 %copy-start = (bf16[1024,1024]{1,0:T(8,128)(2,1)S(1)}, bf16[1024,1024]{1,0:T(8,128)(2,1)}, u32[]{:S(2)}) copy-start(bf16[1024,1024]{1,0:T(8,128)(2,1)} %copy.46.w_k_hbm) | copy-start | bytes 6291460
  72.6 11.7 %copy-start.1 = (bf16[1024,1024]{1,0:T(8,128)(2,1)S(1)}, bf16[1024,1024]{1,0:T(8,128)(2,1)}, u32[]{:S(2)}) copy-start(bf16[1024,1024]{1,0:T(8,128)(2,1)} %copy.47.w_v_hbm) | copy-start | bytes 6291460

commit v2 on v1

v2 whole, which is shorter than its diff:
```python
import jax
import jax.numpy as jnp
from jax import lax
from jax.experimental import pallas as pl
from jax.experimental.pallas import tpu as pltpu
from jax.sharding import PartitionSpec as P

WIN = 128
TILE = 256
CHUNK = 256
BIG = 1 << 20
NEG = -1e30
F32 = jnp.float32
BF16 = jnp.bfloat16
VMEM = pl.BlockSpec(memory_space=pltpu.VMEM)
SMEM = pl.BlockSpec(memory_space=pltpu.SMEM)
HBM = pl.BlockSpec(memory_space=pltpu.HBM)
MEGA = 1 << 20
REMOTE_LIMIT = 44
INNER_LIMIT = 39


def dot(a, b):
    return jnp.dot(a, b, preferred_element_type=F32)


def dot_nt(a, b):
    return lax.dot_general(a, b, (((1,), (1,)), ((), ())), preferred_element_type=F32)


def onehot(index, size):
    place = lax.broadcasted_iota(jnp.int32, (CHUNK, index.shape[1]), 0).astype(F32).astype(BF16)
    parts = []
    for start in range(0, size, CHUNK):
        at = jnp.broadcast_to((index - start).astype(F32).astype(BF16), place.shape)
        parts.append(jnp.where(place == at, jnp.ones_like(place), jnp.zeros_like(place)))
    return parts[0] if len(parts) == 1 else jnp.concatenate(parts, axis=0)


def start_all(pairs, sems):
    copies = [pltpu.make_async_copy(a, b, sems.at[i]) for i, (a, b) in enumerate(pairs)]
    for copy in copies:
        copy.start()
    return copies


def rms_scale(values, gain):
    mean_sq = jnp.mean(values * values, axis=-1, keepdims=True)
    return values * lax.rsqrt(mean_sq + 1e-05) * gain


def send_kernel(x_hbm, w_hbm, halo_hbm, table_hbm, out_hbm, x_ref, w_ref, halo_ref, table_ref, out_ref, in_sems, out_sems):
    rows, width = x_ref.shape
    parts = 4
    step = width // parts
    pairs = []
    for part in range(parts):
        cols = pl.ds(part * step, step)
        pairs.append((x_hbm.at[:, cols], x_ref.at[:, cols]))
        pairs.append((w_hbm.at[cols], w_ref.at[cols]))
    pairs.append((halo_hbm, halo_ref))
    copies = start_all(pairs, in_sems)
    proj = None
    for part in range(parts):
        copies[2 * part].wait()
        copies[2 * part + 1].wait()
        piece = dot(x_ref[:, part * step : (part + 1) * step], w_ref[part * step : (part + 1) * step])
        proj = piece if proj is None else proj + piece
    proj_t = jnp.transpose(proj).astype(BF16)
    for part in range(table_ref.shape[0]):
        table_ref[part] = proj_t[:, part * 128 : (part + 1) * 128]
    writes = [pltpu.make_async_copy(table_ref, table_hbm, out_sems.at[0])]
    writes[0].start()
    copies[2 * parts].wait()
    for pair in range(out_ref.shape[0] // 2):
        hot = jnp.concatenate(
            [onehot(halo_ref[pl.ds(2 * pair + k, 1), :], rows) for k in range(2)], axis=1
        )
        picked = dot(proj_t, hot).astype(BF16)
        out_ref[2 * pair] = picked[:, :128]
        out_ref[2 * pair + 1] = picked[:, 128:]
        two = pl.ds(2 * pair, 2)
        writes.append(pltpu.make_async_copy(out_ref.at[two], out_hbm.at[two], out_sems.at[1 + pair]))
        writes[-1].start()
    for write in writes:
        write.wait()


def edge_tiles(span, chunks, flat_ref, keys_ref, table_ref, recv_ref, bias_ref, pre_ref, hot_ref, agg_ref):
    rows = recv_ref.shape[1]
    begin, end = chunks

    def chunk_of(index, slot):
        at = 2 * (index - begin)
        chunk = jnp.concatenate([table_ref[at], table_ref[at + 1]], axis=1)
        return dot(chunk, onehot(slot - index * CHUNK, CHUNK))

    def indices(tile):
        key = keys_ref[tile]
        chunk = key >> 17
        slot = (chunk << 8) | (key & 255)
        recv = jnp.where((chunk >= begin) & (chunk < end), (key >> 8) & 511, -1)
        return recv, slot

    def gather(tile, place):
        recv, slot = indices(tile)
        low = jnp.maximum(flat_ref[tile * TILE] >> 17, begin)
        low = jnp.minimum(low, end - 2)
        hot = onehot(recv, rows)
        hot_ref[place] = hot
        pre_ref[place] = (
            dot(recv_ref[...], hot)
            + (chunk_of(low, slot) + chunk_of(low + 1, slot))
            + jnp.concatenate([bias_ref[...]] * (TILE // 128), axis=1)
        )

    def rest(tile, place):
        if end - begin > 2:
            slot = indices(tile)[1]
            low = jnp.minimum(jnp.maximum(flat_ref[tile * TILE] >> 17, begin), end - 2)
            high = jnp.minimum(flat_ref[tile * TILE + TILE - 1] >> 17, end - 1)

            def more(index, inner):
                pre_ref[place] += chunk_of(index, slot)
                return inner

            lax.fori_loop(low + 2, high + 1, more, 0)

    def scatter(place):
        half = 0.5 * pre_ref[place]
        message = (half + half * jnp.tanh(half)).astype(BF16)
        agg_ref[...] += dot_nt(hot_ref[place], message)

    start, stop = span

    @pl.when(start < stop)
    def _():
        gather(start, 0)
        rest(start, 0)

    def body(tile, carry):
        def step(now, later):
            scatter(now)
            gather(tile, later)
            rest(tile, later)

        odd = (tile - start) & 1
        pl.when(odd == 1)(lambda: step(0, 1))
        pl.when(odd == 0)(lambda: step(1, 0))
        return carry

    lax.fori_loop(start + 1, stop, body, 0)

    @pl.when(start < stop)
    def _():
        scatter((stop - 1 - start) & 1)


def tiles_of(flat_ref, tiles, bound):
    def count(tile, total):
        first = jnp.where((flat_ref[tile * TILE] >> 17) < bound, 1, 0)
        last = jnp.where((flat_ref[tile * TILE + TILE - 1] >> 17) < bound, 1, 0)
        return total[0] + first, total[1] + last

    return lax.fori_loop(0, tiles, count, (0, 0))


def local_kernel(
    flat_ref,
    keys_ref,
    bias_ref,
    x_hbm,
    w_hbm,
    table_hbm,
    w_message_hbm,
    w_lift_hbm,
    mats_hbm,
    agg_hbm,
    wide_hbm,
    x_ref,
    w_ref,
    table_ref,
    recv_ref,
    agg_ref,
    w_message_ref,
    w_lift_ref,
    pre_ref,
    hot_ref,
    bias_wide,
    sems,
):
    copies = start_all(
        [
            (x_hbm, x_ref),
            (w_hbm, w_ref),
            (table_hbm, table_ref),
            (w_message_hbm, w_message_ref),
            (w_lift_hbm, w_lift_ref),
        ],
        sems,
    )
    bias_wide[...] = jnp.transpose(jnp.broadcast_to(bias_ref[...], bias_wide.shape[::-1]))
    agg_ref[...] = jnp.zeros_like(agg_ref)
    copies[0].wait()
    copies[1].wait()
    proj = dot(x_ref[...], w_ref[...])
    recv_ref[...] = jnp.transpose(proj).astype(BF16)
    for copy in copies[2:]:
        copy.wait()
    early = start_all(
        [
            (recv_ref, mats_hbm.at[0]),
            (w_message_ref, mats_hbm.at[1]),
            (w_lift_ref, wide_hbm.at[0]),
            (x_ref, wide_hbm.at[1]),
        ],
        sems.at[pl.ds(6, 4)],
    )
    own = x_ref.shape[0] // CHUNK
    split = tiles_of(flat_ref, keys_ref.shape[0], own)[0]
    edge_tiles(
        (0, split), (0, own), flat_ref, keys_ref, table_ref, recv_ref, bias_wide, pre_ref, hot_ref, agg_ref
    )
    late = pltpu.make_async_copy(agg_ref, agg_hbm.at[0], sems.at[5])
    late.start()
    for copy in early:
        copy.wait()
    late.wait()


def finish_rows(agg, x, w_message, msg_gain, w_lift, attn_gain):
    high = agg.astype(BF16)
    low = (agg - high.astype(F32)).astype(BF16)
    mixed = dot(high, w_message) + dot(low, w_message)
    normed = rms_scale(mixed, msg_gain).astype(BF16)
    state = (x.astype(F32) + dot(normed, w_lift)).astype(BF16)
    return state, rms_scale(state.astype(F32), attn_gain).astype(BF16)


def remote_kernel(
    flat_ref,
    keys_ref,
    bias_ref,
    msg_gain_ref,
    attn_gain_ref,
    come_ref,
    mats_hbm,
    agg_hbm,
    wide_hbm,
    w_qkv_hbm,
    state_ref,
    attn_ref,
    top_ref,
    bottom_ref,
    w_q_ref,
    recv_ref,
    agg_in_ref,
    x_ref,
    w_message_ref,
    w_lift_ref,
    agg_ref,
    pre_ref,
    hot_ref,
    bias_wide,
    sems,
):
    rows = agg_ref.shape[0]
    first = pltpu.make_async_copy(mats_hbm.at[0], recv_ref, sems.at[0])
    first.start()
    agg_ref[...] = jnp.zeros_like(agg_ref)
    bias_wide[...] = jnp.transpose(jnp.broadcast_to(bias_ref[...], bias_wide.shape[::-1]))
    tiles = keys_ref.shape[0]
    own = rows // CHUNK
    split = tiles_of(flat_ref, tiles, own)[1]
    first.wait()
    later = start_all(
        [
            (agg_hbm.at[0], agg_in_ref),
            (mats_hbm.at[1], w_message_ref),
            (wide_hbm.at[0], w_lift_ref),
            (wide_hbm.at[1], x_ref),
            (w_qkv_hbm.at[:, pl.ds(0, w_q_ref.shape[1])], w_q_ref),
        ],
        sems.at[pl.ds(1, 5)],
    )
    edge_tiles(
        (split, tiles),
        (own, own + come_ref.shape[0] // 2),
        flat_ref,
        keys_ref,
        come_ref,
        recv_ref,
        bias_wide,
        pre_ref,
        hot_ref,
        agg_ref,
    )
    for copy in later:
        copy.wait()
    state, attn_in = finish_rows(
        agg_ref[...] + agg_in_ref[...],
        x_ref[...],
        w_message_ref[...],
        msg_gain_ref[...],
        w_lift_ref[...],
        attn_gain_ref[...],
    )
    state_ref[...] = state
    attn_ref[...] = attn_in
    top_ref[...] = attn_in[:WIN]
    bottom_ref[...] = attn_in[rows - WIN :]


def attend(q, k, v, apart, reach):
    lane = lax.broadcasted_iota(jnp.int32, q.shape, 1)
    zero = jnp.zeros_like(q)
    both = jnp.concatenate([jnp.where(lane < 64, q, zero), jnp.where(lane >= 64, q, zero)], axis=0)
    score = dot_nt(both, k)
    parts = []
    rows = q.shape[0]
    for head in range(2):
        one = score[head * rows : (head + 1) * rows]
        one = jnp.where(apart <= reach[head], one, NEG)
        top = jnp.max(one, axis=-1, keepdims=True)
        parts.append(jnp.exp2(one - top).astype(BF16))
    weights = jnp.concatenate(parts, axis=0)
    wide = jnp.concatenate([v, jnp.ones((v.shape[0], 128), BF16)], axis=1)
    mixed = dot(weights, wide)
    out = mixed[:, :128] / mixed[:, 128:]
    return jnp.where(lane < 64, out[:rows], out[rows:]).astype(BF16)


def distance(rows, keys):
    q_at = lax.broadcasted_iota(jnp.int32, (rows, keys), 0) + WIN
    k_at = lax.broadcasted_iota(jnp.int32, (rows, keys), 1)
    return jnp.abs(q_at - k_at), k_at


LOG2E = 1.4426950408889634


def project(rows, w_ref, scale=None):
    heads, size, width = w_ref.shape
    out = dot_nt(rows, w_ref[...].reshape(heads * size, width))
    return (out if scale is None else out * scale).astype(BF16)


def inner_kernel(
    reach_ref,
    state_ref,
    attn_ref,
    w_q_ref,
    w_qkv_hbm,
    w_out_hbm,
    q_ref,
    k_ref,
    v_ref,
    res_ref,
    w_k_ref,
    w_v_ref,
    w_out_ref,
    q_mid,
    mix_ref,
    apart_ref,
    sems,
):
    rows = attn_ref.shape[0]
    mid = rows - 2 * WIN
    size = w_k_ref.shape[1]
    copies = start_all(
        [
            (w_qkv_hbm.at[:, pl.ds(size, size)], w_k_ref),
            (w_qkv_hbm.at[:, pl.ds(2 * size, size)], w_v_ref),
            (w_out_hbm, w_out_ref),
        ],
        sems,
    )
    apart_ref[...] = distance(WIN, 3 * WIN)[0]
    q = project(attn_ref[...], w_q_ref, size**-0.5 * LOG2E)
    q_ref[pl.ds(0, WIN), :] = q[:WIN]
    q_ref[pl.ds(WIN, WIN), :] = q[rows - WIN :]
    q_mid[...] = q[WIN : rows - WIN]
    copies[0].wait()
    k_ref[...] = project(attn_ref[...], w_k_ref)
    copies[1].wait()
    v_ref[...] = project(attn_ref[...], w_v_ref)

    def body(pair, carry):
        lanes = pl.ds(pl.multiple_of(pair * 128, 128), 128)
        reach = (reach_ref[2 * pair], reach_ref[2 * pair + 1])
        for block in range(2):
            keys = pl.ds(block * WIN, 3 * WIN)
            mix_ref[pl.ds(block * WIN, WIN), lanes] = attend(
                q_mid[pl.ds(block * WIN, WIN), lanes],
                k_ref[keys, lanes],
                v_ref[keys, lanes],
                apart_ref[...],
                reach,
            )
        return carry

    lax.fori_loop(0, q_ref.shape[1] // 128, body, 0, unroll=8)
    copies[2].wait()
    res_ref[...] = (state_ref[pl.ds(WIN, mid), :].astype(F32) + dot(mix_ref[...], w_out_ref[...])).astype(BF16)


def outer_kernel(
    reach_ref,
    q_ref,
    left_ref,
    right_ref,
    k_ref,
    v_ref,
    state_ref,
    res_ref,
    w_k_ref,
    w_v_ref,
    w_out_ref,
    out_hbm,
    keys_ref,
    values_ref,
    apart_ref,
    mix_ref,
    fin_ref,
    sems,
):
    rows = k_ref.shape[0]
    early = pltpu.make_async_copy(res_ref, out_hbm.at[pl.ds(WIN, rows - 2 * WIN)], sems.at[0])
    early.start()
    me = lax.axis_index("node")
    last = lax.axis_size("node") - 1
    halo = jnp.concatenate([left_ref[...], right_ref[...]], axis=0)
    two = 2 * WIN
    keys_ref[0, pl.ds(WIN, two), :] = k_ref[pl.ds(0, two), :]
    keys_ref[1, pl.ds(0, two), :] = k_ref[pl.ds(rows - two, two), :]
    values_ref[0, pl.ds(WIN, two), :] = v_ref[pl.ds(0, two), :]
    values_ref[1, pl.ds(0, two), :] = v_ref[pl.ds(rows - two, two), :]
    apart, k_at = distance(WIN, 3 * WIN)
    apart_ref[0] = jnp.where((k_at < WIN) & (me == 0), BIG, apart)
    apart_ref[1] = jnp.where((k_at >= two) & (me == last), BIG, apart)
    k_halo = project(halo, w_k_ref)
    keys_ref[0, pl.ds(0, WIN), :] = k_halo[:WIN]
    keys_ref[1, pl.ds(two, WIN), :] = k_halo[WIN:]
    v_halo = project(halo, w_v_ref)
    values_ref[0, pl.ds(0, WIN), :] = v_halo[:WIN]
    values_ref[1, pl.ds(two, WIN), :] = v_halo[WIN:]

    def body(pair, carry):
        lanes = pl.ds(pl.multiple_of(pair * 128, 128), 128)
        reach = (reach_ref[2 * pair], reach_ref[2 * pair + 1])
        for block in range(2):
            mix_ref[pl.ds(block * WIN, WIN), lanes] = attend(
                q_ref[pl.ds(block * WIN, WIN), lanes],
                keys_ref[block, :, lanes],
                values_ref[block, :, lanes],
                apart_ref[block],
                reach,
            )
        return carry

    lax.fori_loop(0, q_ref.shape[1] // 128, body, 0, unroll=8)
    state = jnp.concatenate([state_ref[:WIN], state_ref[rows - WIN :]], axis=0)
    fin_ref[...] = (state.astype(F32) + dot(mix_ref[...], w_out_ref[...])).astype(BF16)
    ends = [
        pltpu.make_async_copy(fin_ref.at[pl.ds(0, WIN)], out_hbm.at[pl.ds(0, WIN)], sems.at[1]),
        pltpu.make_async_copy(
            fin_ref.at[pl.ds(WIN, WIN)], out_hbm.at[pl.ds(rows - WIN, WIN)], sems.at[2]
        ),
    ]
    for copy in ends:
        copy.start()
    early.wait()
    for copy in ends:
        copy.wait()


def call(kernel, name, out_shape, in_specs, out_specs, scratch, flops, moved, limit):
    return pl.pallas_call(
        kernel,
        name=name,
        out_shape=out_shape,
        in_specs=in_specs,
        out_specs=out_specs,
        scratch_shapes=scratch,
        compiler_params=pltpu.CompilerParams(vmem_limit_bytes=limit * MEGA),
        cost_estimate=pl.CostEstimate(flops=flops, bytes_accessed=moved, transcendentals=0),
    )


def local(
    node_state,
    edge_recv,
    edge_send,
    halo_rows,
    window_reach,
    w_recv,
    w_send,
    edge_bias,
    w_message,
    msg_gain,
    w_lift,
    attn_gain,
    w_qkv,
    w_out,
):
    shape = jax.ShapeDtypeStruct
    rows, width = node_state.shape
    hidden = w_recv.shape[1]
    peers, halo = halo_rows.shape[1:]
    edges = edge_recv.shape[0]
    tiles = edges // TILE
    dma = pltpu.SemaphoreType.DMA

    table, outgoing = call(
        send_kernel,
        "send",
        (shape((rows // 128, hidden, 128), BF16), shape((peers, hidden, halo), BF16)),
        [HBM] * 3,
        (HBM, HBM),
        [
            pltpu.VMEM((rows, width), BF16),
            pltpu.VMEM((width, hidden), BF16),
            pltpu.VMEM((peers, halo), jnp.int32),
            pltpu.VMEM((rows // 128, hidden, 128), BF16),
            pltpu.VMEM((peers, hidden, halo), BF16),
            dma((9,)),
            dma((1 + peers // 2,)),
        ],
        4 << 30,
        4 * MEGA,
        60,
    )(node_state, w_send, halo_rows.reshape(peers, halo))
    incoming = lax.all_to_all(outgoing, "node", split_axis=0, concat_axis=0, tiled=True)

    flat = lax.sort(((edge_send >> 8) << 17) | (edge_recv << 8) | (edge_send & 255))
    keys = flat.reshape(tiles, 1, TILE)
    bias = edge_bias.reshape(1, hidden)
    mats, agg, wide = call(
        local_kernel,
        "local_edges",
        (
            shape((16, hidden, rows), BF16),
            shape((8, rows, hidden), F32),
            shape((8, rows, width), BF16),
        ),
        [SMEM] + [VMEM] * 2 + [HBM] * 5,
        (HBM,) * 3,
        [
            pltpu.VMEM((rows, width), BF16),
            pltpu.VMEM((width, hidden), BF16),
            pltpu.VMEM((rows // 128, hidden, 128), BF16),
            pltpu.VMEM((hidden, rows), BF16),
            pltpu.VMEM((rows, hidden), F32),
            pltpu.VMEM((hidden, hidden), BF16),
            pltpu.VMEM((hidden, width), BF16),
            pltpu.VMEM((2, hidden, TILE), F32),
            pltpu.VMEM((2, rows, TILE), BF16),
            pltpu.VMEM((hidden, 128), F32),
            dma((10,)),
        ],
        10 << 30,
        4 * MEGA,
        60,
    )(flat, keys, bias, node_state, w_recv, table, w_message, w_lift)
    w_qkv_t = jnp.transpose(w_qkv, (1, 2, 0))

    gain_m = msg_gain.reshape(1, hidden)
    gain_a = attn_gain.reshape(1, width)
    heads = w_qkv.shape[1]
    part = (heads, width // heads, width)
    state, attn_in, top, bottom, w_q = call(
        remote_kernel,
        "remote_edges",
        (
            shape((rows, width), BF16),
            shape((rows, width), BF16),
            shape((WIN, width), BF16),
            shape((WIN, width), BF16),
            shape(part, BF16),
        ),
        [SMEM] + [VMEM] * 5 + [HBM] * 4,
        (VMEM,) * 5,
        [
            pltpu.VMEM((hidden, rows), BF16),
            pltpu.VMEM((rows, hidden), F32),
            pltpu.VMEM((rows, width), BF16),
            pltpu.VMEM((hidden, hidden), BF16),
            pltpu.VMEM((hidden, width), BF16),
            pltpu.VMEM((rows, hidden), F32),
            pltpu.VMEM((2, hidden, TILE), F32),
            pltpu.VMEM((2, rows, TILE), BF16),
            pltpu.VMEM((hidden, 128), F32),
            dma((6,)),
        ],
        10 << 30,
        4 * MEGA,
        REMOTE_LIMIT,
    )(flat, keys, bias, gain_m, gain_a, incoming, mats, agg, wide, w_qkv_t)

    nodes = lax.axis_size("node")
    left = lax.ppermute(bottom, "node", [(i, (i + 1) % nodes) for i in range(nodes)])
    right = lax.ppermute(top, "node", [(i, (i - 1) % nodes) for i in range(nodes)])

    q_tb, k, v, res_mid, *rest = call(
        inner_kernel,
        "inner",
        (
            shape((2 * WIN, width), BF16),
            shape((rows, width), BF16),
            shape((rows, width), BF16),
            shape((rows - 2 * WIN, width), BF16),
            shape(part, BF16),
            shape(part, BF16),
            shape(w_out.shape, BF16),
        ),
        [SMEM] + [VMEM] * 3 + [HBM] * 2,
        (VMEM,) * 7,
        [
            pltpu.VMEM((rows - 2 * WIN, width), BF16),
            pltpu.VMEM((rows - 2 * WIN, width), BF16),
            pltpu.VMEM((WIN, 3 * WIN), jnp.int32),
            dma((3,)),
        ],
        10 << 30,
        12 * MEGA,
        INNER_LIMIT,
    )(window_reach, state, attn_in, w_q, w_qkv_t, w_out)

    return call(
        outer_kernel,
        "outer",
        shape((rows, width), BF16),
        [SMEM] + [VMEM] * 10,
        HBM,
        [
            pltpu.VMEM((2, 3 * WIN, width), BF16),
            pltpu.VMEM((2, 3 * WIN, width), BF16),
            pltpu.VMEM((2, WIN, 3 * WIN), jnp.int32),
            pltpu.VMEM((2 * WIN, width), BF16),
            pltpu.VMEM((2 * WIN, width), BF16),
            dma((3,)),
        ],
        6 << 30,
        12 * MEGA,
        24,
    )(window_reach, q_tb, left, right, k, v, state, res_mid, *rest)


def solution(mesh):
    split = ("dp", "node")
    in_specs = (P(split, None), P(split), P(split), P(split, None, None)) + (P(),) * 10
    return jax.shard_map(
        local, mesh=mesh, in_specs=in_specs, out_specs=P(split, None), check_vma=False
    )
```

time: 94.7 us -> 73.4 us (0.78)
  local copies, waits for them, and re-layouts: 34.5 us -> 0.04 us
  waiting for transfers between devices: 0.01 us -> 14.9 us
    unnamed x52 -> x14, local copies, waits for them, and re-layouts: 16.2 us -> 0.03 us
    all_to_all x1, waiting for transfers between devices: 0.01 us -> 14.9 us  [local(): lax.all_to_all(outgoing, 'node', split_axis=0, concat_axis=0, tiled=True)]
    another operation x3 -> x0, local copies, waits for them, and re-layouts: 11.9 us -> none  [local(): split_qkv[:, :, i].reshape(width, heads * size)]
    slice x4 -> x0, local copies, waits for them, and re-layouts: 6.04 us -> none  [the longest x1 5.8 us: local(): split_qkv[:, :, i].reshape(width, heads * size)]
    pallas_call x1, Pallas kernels: 11.6 us -> 9.07 us  [local(): call(inner_kernel, 'inner', (shape((2 * WIN, width), BF16), shape((rows,...]
    pallas_call x1, Pallas kernels: 9.35 us -> 6.87 us  [local(): call(outer_kernel, 'outer', shape((rows, width), BF16), [SMEM] + [VMEM] *...]
    pallas_call x1, Pallas kernels: 1.92 us -> 4.35 us  [local(): call(send_kernel, 'send', (shape((rows // 128, hidden, 128), BF16), shape...]
    ppermute x1, starting transfers between devices: 1.98 us -> 0.08 us  [local(): lax.ppermute(bottom, 'node', [(i, (i + 1) % nodes) for i in range(nodes)])]
  transfers between devices with their start and end apart: 3 -> 3, of which waited for: 0 -> 1; matrix products, arithmetic and copies ran while one was open for 26% -> 8% of each run, Pallas kernels for 21% -> 27%
where the time goes in v2:
time: 73.4 us; the launch traced here: 73.1 us
  Pallas kernels  39.6 us (54%)
  waiting for transfers between devices  14.9 us (20%)
  starting transfers between devices  12.5 us (17%)
  other arithmetic  5.79 us (8%)
    all_to_all x1, waiting for transfers between devices, local(): lax.all_to_all(outgoing, 'node', split_axis=0, concat_axis=0, tiled=True)  14.9 us
    pallas_call x1, Pallas kernels, local(): call(local_kernel, 'local_edges', (shape((16, hidden, rows), BF16), shape...  10.9 us
    pallas_call x1, Pallas kernels, local(): call(inner_kernel, 'inner', (shape((2 * WIN, width), BF16), shape((rows,...  9.07 us
    pallas_call x1, Pallas kernels, local(): call(remote_kernel, 'remote_edges', (shape((rows, width), BF16), shape((r...  8.35 us
    all_to_all x1, starting transfers between devices, local(): lax.all_to_all(outgoing, 'node', split_axis=0, concat_axis=0, tiled=True)  7.04 us
    pallas_call x1, Pallas kernels, local(): call(outer_kernel, 'outer', shape((rows, width), BF16), [SMEM] + [VMEM] *...  6.87 us
    sort x1, other arithmetic, local(): flat = lax.sort(edge_send >> 8 << 17 | edge_recv << 8 | edge_send & 255)  5.78 us
    ppermute x1, starting transfers between devices, local(): lax.ppermute(top, 'node', [(i, (i - 1) % nodes) for i in range(nodes)])  5.33 us
  transfers between devices with their start and end apart: 3, of which 1 were waited for; matrix products, arithmetic and copies ran while one was open for 8% of the time, Pallas kernels for 27%

profile of v2, /device:TPU:224, one launch (start us, length us, event | category | flops | bytes accessed | tf_op | source)
XLA Modules:
  0.0 73.1 jit_solution(5155322827855836885)
XLA Ops:
  0.0 4.3 %send.1 = (bf16[4,512,128]{2,1,0:T(8,128)(2,1)}, bf16[16,512,128]{2,1,0:T(8,128)(2,1)}) custom-call(bf16[512,1024]{1,0:T(8,128)(2,1)} %x_hbm.3, bf16[1024,512]{1,0:T(8,128)(2,1)} %w_hbm.2, s32[16,128]{1,0:T(8,128)} %bitcast.14), custom_call_target="tpu_custom_call" | custom-call | flops 4294967296 | bytes 4194304 | tf_op jit(solution)/shard_map/send/pallas_call | solution.py:514
  4.4 0.0 copy-start.5
  4.4 0.0 copy-start.6
  4.4 7.0 %all-to-all-start = ((bf16[16,512,128]{2,1,0:T(8,128)(2,1)}), bf16[16,512,128]{2,1,0:T(8,128)(2,1)S(1)}, u32[]{:S(2)}, u32[]{:S(2)}) async-start(bf16[16,512,128]{2,1,0:T(8,128)(2,1)} %get-tuple-element.25), calls=%async_computation | async-start | bytes 4194304 | tf_op jit(solution)/shard_map/all_to_all | solution.py:533
  11.4 0.0 copy-done.5
  11.4 0.0 copy-done.6
  11.5 5.8 %sort.10 = (s32[4096]{0:T(1024)}, s32[4096]{0:T(1024)}) sort(s32[4096]{0:T(1024)S(1)} %and_or_fusion, s32[4096]{0:T(1024)S(1)} %iota.3), dimensions={0}, to_apply=%region_0.0 | sort | flops 49152 | bytes 65536 | tf_op jit(solution)/shard_map/sort | solution.py:535
  17.2 0.0 copy-start
  17.3 0.0 copy-start.1
  17.3 0.0 copy-start.2
  17.3 0.0 copy-start.3
  17.3 10.9 %local_edges.1 = (bf16[16,512,512]{2,1,0:T(8,128)(2,1)}, f32[8,512,512]{2,1,0:T(8,128)}, bf16[8,512,1024]{2,1,0:T(8,128)(2,1)}) custom-call(s32[4096]{0:T(1024)} %get-tuple-element.24.flat_ref, s32[16,1,256]{2,1,0:T(1,128)} %bitcast.6, f32[1,512]{1,0:T(1,128)} %bitcast.9, bf16[512,1024]{1,0:T(8,128)(2,1)} %x_hbm.3, bf16[1024,512]{1,0:T(8,128)(2,1)} %w_hbm.3, ...), custom_call_target="tpu_custom_call" | custom-call | flops 10737418240 | bytes 4194304 | tf_op jit(solution)/shard_map/local_edges/pallas_call | solution.py:538
  28.2 14.9 %all-to-all-done.come_ref = bf16[16,512,128]{2,1,0:T(8,128)(2,1)S(1)} async-done(((bf16[16,512,128]{2,1,0:T(8,128)(2,1)}), bf16[16,512,128]{2,1,0:T(8,128)(2,1)S(1)}, u32[]{:S(2)}, u32[]{:S(2)}) %all-to-all-start) | async-done | bytes 2097184 | tf_op jit(solution)/shard_map/all_to_all | solution.py:533
  43.1 0.0 copy-done
  43.1 0.0 copy-done.1
  43.1 0.0 copy-done.2
  43.1 0.0 copy-done.3
  43.1 0.0 copy-start.4
  43.1 8.4 %remote_edges.1 = (bf16[512,1024]{1,0:T(8,128)(2,1)S(1)}, bf16[512,1024]{1,0:T(8,128)(2,1)S(1)}, bf16[128,1024]{1,0:T(8,128)(2,1)S(1)}, bf16[128,1024]{1,0:T(8,128)(2,1)S(1)}, bf16[16,64,1024]{2,1,0:T(8,128)(2,1)S(1)}) custom-call(s32[4096]{0:T(1024)S(1)} %copy-done, s32[16,1,256]{2,1,0:T(1,128)S(1)} %bitcast.7, f32[1,512]{1,0:T(1,128)S(1)} %bitcast.10, ...), custom_call_target="tpu_custom_call" | custom-call | flops 10737418240 | bytes 4194304 | tf_op jit(solution)/shard_map/remote_edges/pallas_call | solution.py:571
  51.5 0.1 collective-permute-start
  51.6 5.3 %collective-permute-start.1 = (bf16[128,1024]{1,0:T(8,128)(2,1)S(1)}, bf16[128,1024]{1,0:T(8,128)(2,1)S(1)}, u32[]{:S(2)}, u32[]{:S(2)}) collective-permute-start(bf16[128,1024]{1,0:T(8,128)(2,1)S(1)} %get-tuple-element.35), channel_id=1, source_target_pairs={{0,15},{1,0},{2,1},{3,2},{4,3},{5,4},{6,5},{7,6},{8,7},{9,8},{10,9... | collective-permute-start | bytes 786440 | tf_op jit(solution)/shard_map/ppermute | solution.py:602
  56.9 0.0 copy-done.4
  56.9 9.1 %inner.1 = (bf16[256,1024]{1,0:T(8,128)(2,1)S(1)}, bf16[512,1024]{1,0:T(8,128)(2,1)S(1)}, bf16[512,1024]{1,0:T(8,128)(2,1)S(1)}, bf16[256,1024]{1,0:T(8,128)(2,1...) custom-call(s32[16]{0:T(128)S(1)} %copy-done.4, ...), custom_call_target="tpu_custom_call" | custom-call | flops 10737418240 | bytes 12582912 | tf_op jit(solution)/shard_map/inner/pallas_call | solution.py:604
  66.0 0.0 collective-permute-done.left_ref
  66.0 0.0 collective-permute-done.1.right_ref
  66.0 6.9 %outer.1 = bf16[512,1024]{1,0:T(8,128)(2,1)} custom-call(s32[16]{0:T(128)S(1)} %copy-done.4, bf16[256,1024]{1,0:T(8,128)(2,1)S(1)} %get-tuple-element.33.q_ref, bf16[128,1024]{1,0:T(8,128)(2,1)S(1)} %collective-permute-done.left_ref, bf16[128,1024]{1,0:T(8,128)(2,1)S(1)} %collective-permute-done.1.right_ref, bf16[512,1024]{1,0:T(8,128)(2,1)S(1)} %get-tuple-element.36.k_ref, ...), custom_call_target="tpu_custom_call" | custom-call | flops 6442450944 | bytes 12582912 | tf_op jit(solution)/shard_map/outer/pallas_call | solution.py:629
  (2 shorter events, 0.0 us)
Async XLA Ops:
  4.4 7.1 %copy-start.5 = (s32[4096]{0:T(1024)S(1)}, s32[4096]{0:T(1024)}, u32[]{:S(2)}) copy-start(s32[4096]{0:T(1024)} %param.16) | copy-start | bytes 49156
  4.4 7.1 %copy-start.6 = (s32[4096]{0:T(1024)S(1)}, s32[4096]{0:T(1024)}, u32[]{:S(2)}) copy-start(s32[4096]{0:T(1024)} %param.15) | copy-start | bytes 49156
  4.4 38.7 %all-to-all-start = ((bf16[16,512,128]{2,1,0:T(8,128)(2,1)}), bf16[16,512,128]{2,1,0:T(8,128)(2,1)S(1)}, u32[]{:S(2)}, u32[]{:S(2)}) async-start(bf16[16,512,128]{2,1,0:T(8,128)(2,1)} %get-tuple-element.25), calls=%async_computation | async-start | bytes 4194304 | tf_op jit(solution)/shard_map/all_to_all | solution.py:533
  17.2 25.9 %copy-start = (s32[4096]{0:T(1024)S(1)}, s32[4096]{0:T(1024)}, u32[]{:S(2)}) copy-start(s32[4096]{0:T(1024)} %get-tuple-element.24.flat_ref) | copy-start | bytes 49156
  17.3 25.9 %copy-start.1 = (f32[1024]{0:T(1024)S(1)}, f32[1024]{0:T(1024)}, u32[]{:S(2)}) copy-start(f32[1024]{0:T(1024)} %param.25) | copy-start | bytes 12292
  17.3 25.9 %copy-start.2 = (f32[512]{0:T(512)S(1)}, f32[512]{0:T(512)}, u32[]{:S(2)}) copy-start(f32[512]{0:T(512)} %param.21) | copy-start | bytes 6148
  17.3 25.9 %copy-start.3 = (f32[512]{0:T(512)S(1)}, f32[512]{0:T(512)}, u32[]{:S(2)}) copy-start(f32[512]{0:T(512)} %param.23) | copy-start | bytes 6148
  43.1 13.8 %copy-start.4 = (s32[16]{0:T(128)S(1)}, s32[16]{0:T(128)}, u32[]{:S(2)}) copy-start(s32[16]{0:T(128)} %reach_ref.3) | copy-start | bytes 196
  51.5 14.5 %collective-permute-start = (bf16[128,1024]{1,0:T(8,128)(2,1)S(1)}, bf16[128,1024]{1,0:T(8,128)(2,1)S(1)}, u32[]{:S(2)}, u32[]{:S(2)}) collective-permute-start(bf16[128,1024]{1,0:T(8,128)(2,1)S(1)} %get-tuple-element.34), channel_id=1, source_target_pairs={{0,1},{1,2},{2,3},{3,4},{4,5},{5,6},{6,7},{7,8},{8,9},{9,10},{10,1... | collective-permute-start | bytes 786440 | tf_op jit(solution)/shard_map/ppermute | solution.py:601
  51.6 14.4 %collective-permute-start.1 = (bf16[128,1024]{1,0:T(8,128)(2,1)S(1)}, bf16[128,1024]{1,0:T(8,128)(2,1)S(1)}, u32[]{:S(2)}, u32[]{:S(2)}) collective-permute-start(bf16[128,1024]{1,0:T(8,128)(2,1)S(1)} %get-tuple-element.35), channel_id=1, source_target_pairs={{0,15},{1,0},{2,1},{3,2},{4,3},{5,4},{6,5},{7,6},{8,7},{9,8},{10,9... | collective-permute-start | bytes 786440 | tf_op jit(solution)/shard_map/ppermute | solution.py:602

commit v3 on v2

--- a/solution.py
+++ b/solution.py
@@ -250,8 +250,8 @@
     w_qkv_hbm,
     state_ref,
     attn_ref,
+    bottom_ref,
     top_ref,
-    bottom_ref,
     w_q_ref,
     recv_ref,
     agg_in_ref,
@@ -326,8 +326,8 @@
     weights = jnp.concatenate(parts, axis=0)
     wide = jnp.concatenate([v, jnp.ones((v.shape[0], 128), BF16)], axis=1)
     mixed = dot(weights, wide)
-    out = mixed[:, :128] / mixed[:, 128:]
-    return jnp.where(lane < 64, out[:rows], out[rows:]).astype(BF16)
+    mine = jnp.where(jnp.concatenate([lane, lane], axis=1) % 128 < 64, mixed[:rows], mixed[rows:])
+    return (mine[:, :128] / mine[:, 128:]).astype(BF16)
 
 
 def distance(rows, keys):
@@ -407,8 +407,8 @@
 def outer_kernel(
     reach_ref,
     q_ref,
+    right_ref,
     left_ref,
-    right_ref,
     k_ref,
     v_ref,
     state_ref,
@@ -431,19 +431,18 @@
     last = lax.axis_size("node") - 1
     halo = jnp.concatenate([left_ref[...], right_ref[...]], axis=0)
     two = 2 * WIN
-    keys_ref[0, pl.ds(WIN, two), :] = k_ref[pl.ds(0, two), :]
-    keys_ref[1, pl.ds(0, two), :] = k_ref[pl.ds(rows - two, two), :]
-    values_ref[0, pl.ds(WIN, two), :] = v_ref[pl.ds(0, two), :]
-    values_ref[1, pl.ds(0, two), :] = v_ref[pl.ds(rows - two, two), :]
     apart, k_at = distance(WIN, 3 * WIN)
     apart_ref[0] = jnp.where((k_at < WIN) & (me == 0), BIG, apart)
     apart_ref[1] = jnp.where((k_at >= two) & (me == last), BIG, apart)
-    k_halo = project(halo, w_k_ref)
-    keys_ref[0, pl.ds(0, WIN), :] = k_halo[:WIN]
-    keys_ref[1, pl.ds(two, WIN), :] = k_halo[WIN:]
-    v_halo = project(halo, w_v_ref)
-    values_ref[0, pl.ds(0, WIN), :] = v_halo[:WIN]
-    values_ref[1, pl.ds(two, WIN), :] = v_halo[WIN:]
+    keys_ref[...] = project(halo, w_k_ref)
+    values_ref[...] = project(halo, w_v_ref)
+
+    def join(own_ref, halo_ref, block, lanes):
+        if block == 0:
+            parts = [halo_ref[pl.ds(0, WIN), lanes], own_ref[pl.ds(0, two), lanes]]
+        else:
+            parts = [own_ref[pl.ds(rows - two, two), lanes], halo_ref[pl.ds(WIN, WIN), lanes]]
+        return jnp.concatenate(parts, axis=0)
 
     def body(pair, carry):
         lanes = pl.ds(pl.multiple_of(pair * 128, 128), 128)
@@ -451,8 +450,8 @@
         for block in range(2):
             mix_ref[pl.ds(block * WIN, WIN), lanes] = attend(
                 q_ref[pl.ds(block * WIN, WIN), lanes],
-                keys_ref[block, :, lanes],
-                values_ref[block, :, lanes],
+                join(k_ref, keys_ref, block, lanes),
+                join(v_ref, values_ref, block, lanes),
                 apart_ref[block],
                 reach,
             )
@@ -568,7 +567,7 @@
     gain_a = attn_gain.reshape(1, width)
     heads = w_qkv.shape[1]
     part = (heads, width // heads, width)
-    state, attn_in, top, bottom, w_q = call(
+    state, attn_in, bottom, top, w_q = call(
         remote_kernel,
         "remote_edges",
         (
@@ -633,8 +632,8 @@
         [SMEM] + [VMEM] * 10,
         HBM,
         [
-            pltpu.VMEM((2, 3 * WIN, width), BF16),
-            pltpu.VMEM((2, 3 * WIN, width), BF16),
+            pltpu.VMEM((2 * WIN, width), BF16),
+            pltpu.VMEM((2 * WIN, width), BF16),
             pltpu.VMEM((2, WIN, 3 * WIN), jnp.int32),
             pltpu.VMEM((2 * WIN, width), BF16),
             pltpu.VMEM((2 * WIN, width), BF16),
@@ -643,7 +642,7 @@
         6 << 30,
         12 * MEGA,
         24,
-    )(window_reach, q_tb, left, right, k, v, state, res_mid, *rest)
+    )(window_reach, q_tb, right, left, k, v, state, res_mid, *rest)
 
 
 def solution(mesh):

time: 73.4 us -> 70 us (0.954)
  starting transfers between devices: 12.5 us -> 9.14 us
    ppermute x1, starting transfers between devices: 5.33 us -> 0.92 us  [local(): lax.ppermute(top, 'node', [(i, (i - 1) % nodes) for i in range(nodes)])]
    ppermute x1, starting transfers between devices: 0.08 us -> 1.19 us  [local(): lax.ppermute(bottom, 'node', [(i, (i + 1) % nodes) for i in range(nodes)])]
  transfers between devices with their start and end apart: 3 -> 3, of which waited for: 1 -> 1; matrix products, arithmetic and copies ran while one was open for 8% -> 8% of each run, Pallas kernels for 27% -> 29%
where the time goes in v3:
time: 70 us; the launch traced here: 69.7 us
  Pallas kernels  39.6 us (57%)
  waiting for transfers between devices  14.9 us (21%)
  starting transfers between devices  9.14 us (13%)
  other arithmetic  5.79 us (8%)
    all_to_all x1, waiting for transfers between devices, local(): lax.all_to_all(outgoing, 'node', split_axis=0, concat_axis=0, tiled=True)  14.9 us
    pallas_call x1, Pallas kernels, local(): call(local_kernel, 'local_edges', (shape((16, hidden, rows), BF16), shape...  10.9 us
    pallas_call x1, Pallas kernels, local(): call(inner_kernel, 'inner', (shape((2 * WIN, width), BF16), shape((rows,...  9.1 us
    pallas_call x1, Pallas kernels, local(): call(remote_kernel, 'remote_edges', (shape((rows, width), BF16), shape((r...  8.36 us
    all_to_all x1, starting transfers between devices, local(): lax.all_to_all(outgoing, 'node', split_axis=0, concat_axis=0, tiled=True)  7.04 us
    pallas_call x1, Pallas kernels, local(): call(outer_kernel, 'outer', shape((rows, width), BF16), [SMEM] + [VMEM] *...  6.82 us
    sort x1, other arithmetic, local(): flat = lax.sort(edge_send >> 8 << 17 | edge_recv << 8 | edge_send & 255)  5.78 us
    pallas_call x1, Pallas kernels, local(): call(send_kernel, 'send', (shape((rows // 128, hidden, 128), BF16), shape...  4.35 us
  transfers between devices with their start and end apart: 3, of which 1 were waited for; matrix products, arithmetic and copies ran while one was open for 8% of the time, Pallas kernels for 29%

profile of v3, /device:TPU:224, one launch (start us, length us, event | category | flops | bytes accessed | tf_op | source)
XLA Modules:
  0.0 69.7 jit_solution(12832437514873591143)
XLA Ops:
  0.0 4.3 %send.1 = (bf16[4,512,128]{2,1,0:T(8,128)(2,1)}, bf16[16,512,128]{2,1,0:T(8,128)(2,1)}) custom-call(bf16[512,1024]{1,0:T(8,128)(2,1)} %x_hbm.3, bf16[1024,512]{1,0:T(8,128)(2,1)} %w_hbm.2, s32[16,128]{1,0:T(8,128)} %bitcast.14), custom_call_target="tpu_custom_call" | custom-call | flops 4294967296 | bytes 4194304 | tf_op jit(solution)/shard_map/send/pallas_call | solution.py:513
  4.4 0.0 copy-start.5
  4.4 0.0 copy-start.6
  4.4 7.0 %all-to-all-start = ((bf16[16,512,128]{2,1,0:T(8,128)(2,1)}), bf16[16,512,128]{2,1,0:T(8,128)(2,1)S(1)}, u32[]{:S(2)}, u32[]{:S(2)}) async-start(bf16[16,512,128]{2,1,0:T(8,128)(2,1)} %get-tuple-element.25), calls=%async_computation | async-start | bytes 4194304 | tf_op jit(solution)/shard_map/all_to_all | solution.py:532
  11.4 0.0 copy-done.5
  11.4 0.0 copy-done.6
  11.5 5.8 %sort.10 = (s32[4096]{0:T(1024)}, s32[4096]{0:T(1024)}) sort(s32[4096]{0:T(1024)S(1)} %and_or_fusion, s32[4096]{0:T(1024)S(1)} %iota.3), dimensions={0}, to_apply=%region_0.0 | sort | flops 49152 | bytes 65536 | tf_op jit(solution)/shard_map/sort | solution.py:534
  17.2 0.0 copy-start
  17.3 0.0 copy-start.1
  17.3 0.0 copy-start.2
  17.3 0.0 copy-start.3
  17.3 10.9 %local_edges.1 = (bf16[16,512,512]{2,1,0:T(8,128)(2,1)}, f32[8,512,512]{2,1,0:T(8,128)}, bf16[8,512,1024]{2,1,0:T(8,128)(2,1)}) custom-call(s32[4096]{0:T(1024)} %get-tuple-element.24.flat_ref, s32[16,1,256]{2,1,0:T(1,128)} %bitcast.6, f32[1,512]{1,0:T(1,128)} %bitcast.9, bf16[512,1024]{1,0:T(8,128)(2,1)} %x_hbm.3, bf16[1024,512]{1,0:T(8,128)(2,1)} %w_hbm.3, ...), custom_call_target="tpu_custom_call" | custom-call | flops 10737418240 | bytes 4194304 | tf_op jit(solution)/shard_map/local_edges/pallas_call | solution.py:537
  28.2 14.9 %all-to-all-done.come_ref = bf16[16,512,128]{2,1,0:T(8,128)(2,1)S(1)} async-done(((bf16[16,512,128]{2,1,0:T(8,128)(2,1)}), bf16[16,512,128]{2,1,0:T(8,128)(2,1)S(1)}, u32[]{:S(2)}, u32[]{:S(2)}) %all-to-all-start) | async-done | bytes 2097184 | tf_op jit(solution)/shard_map/all_to_all | solution.py:532
  43.1 0.0 copy-done
  43.1 0.0 copy-done.1
  43.1 0.0 copy-done.2
  43.1 0.0 copy-done.3
  43.1 0.0 copy-start.4
  43.1 8.4 %remote_edges.1 = (bf16[512,1024]{1,0:T(8,128)(2,1)S(1)}, bf16[512,1024]{1,0:T(8,128)(2,1)S(1)}, bf16[128,1024]{1,0:T(8,128)(2,1)S(1)}, bf16[128,1024]{1,0:T(8,128)(2,1)S(1)}, bf16[16,64,1024]{2,1,0:T(8,128)(2,1)S(1)}) custom-call(s32[4096]{0:T(1024)S(1)} %copy-done, s32[16,1,256]{2,1,0:T(1,128)S(1)} %bitcast.7, f32[1,512]{1,0:T(1,128)S(1)} %bitcast.10, ...), custom_call_target="tpu_custom_call" | custom-call | flops 10737418240 | bytes 4194304 | tf_op jit(solution)/shard_map/remote_edges/pallas_call | solution.py:570
  51.5 0.9 %collective-permute-start = (bf16[128,1024]{1,0:T(8,128)(2,1)S(1)}, bf16[128,1024]{1,0:T(8,128)(2,1)S(1)}, u32[]{:S(2)}, u32[]{:S(2)}) collective-permute-start(bf16[128,1024]{1,0:T(8,128)(2,1)S(1)} %get-tuple-element.34), channel_id=1, source_target_pairs={{0,15},{1,0},{2,1},{3,2},{4,3},{5,4},{6,5},{7,6},{8,7},{9,8},{10,9... | collective-permute-start | bytes 786440 | tf_op jit(solution)/shard_map/ppermute | solution.py:601
  52.4 1.2 %collective-permute-start.1 = (bf16[128,1024]{1,0:T(8,128)(2,1)S(1)}, bf16[128,1024]{1,0:T(8,128)(2,1)S(1)}, u32[]{:S(2)}, u32[]{:S(2)}) collective-permute-start(bf16[128,1024]{1,0:T(8,128)(2,1)S(1)} %get-tuple-element.35), channel_id=1, source_target_pairs={{0,1},{1,2},{2,3},{3,4},{4,5},{5,6},{6,7},{7,8},{8,9},{9,10},{10,1... | collective-permute-start | bytes 786440 | tf_op jit(solution)/shard_map/ppermute | solution.py:600
  53.6 0.0 copy-done.4
  53.6 9.1 %inner.1 = (bf16[256,1024]{1,0:T(8,128)(2,1)S(1)}, bf16[512,1024]{1,0:T(8,128)(2,1)S(1)}, bf16[512,1024]{1,0:T(8,128)(2,1)S(1)}, bf16[256,1024]{1,0:T(8,128)(2,1...) custom-call(s32[16]{0:T(128)S(1)} %copy-done.4, ...), custom_call_target="tpu_custom_call" | custom-call | flops 10737418240 | bytes 12582912 | tf_op jit(solution)/shard_map/inner/pallas_call | solution.py:603
  62.7 0.0 collective-permute-done.right_ref
  62.7 0.0 collective-permute-done.1.left_ref
  62.7 6.8 %outer.1 = bf16[512,1024]{1,0:T(8,128)(2,1)} custom-call(s32[16]{0:T(128)S(1)} %copy-done.4, bf16[256,1024]{1,0:T(8,128)(2,1)S(1)} %get-tuple-element.33.q_ref, bf16[128,1024]{1,0:T(8,128)(2,1)S(1)} %collective-permute-done.right_ref, bf16[128,1024]{1,0:T(8,128)(2,1)S(1)} %collective-permute-done.1.left_ref, bf16[512,1024]{1,0:T(8,128)(2,1)S(1)} %get-tuple-element.36.k_ref, ...), custom_call_target="tpu_custom_call" | custom-call | flops 6442450944 | bytes 12582912 | tf_op jit(solution)/shard_map/outer/pallas_call | solution.py:628
  (2 shorter events, 0.0 us)
Async XLA Ops:
  4.4 7.1 %copy-start.5 = (s32[4096]{0:T(1024)S(1)}, s32[4096]{0:T(1024)}, u32[]{:S(2)}) copy-start(s32[4096]{0:T(1024)} %param.16) | copy-start | bytes 49156
  4.4 7.1 %copy-start.6 = (s32[4096]{0:T(1024)S(1)}, s32[4096]{0:T(1024)}, u32[]{:S(2)}) copy-start(s32[4096]{0:T(1024)} %param.15) | copy-start | bytes 49156
  4.4 38.7 %all-to-all-start = ((bf16[16,512,128]{2,1,0:T(8,128)(2,1)}), bf16[16,512,128]{2,1,0:T(8,128)(2,1)S(1)}, u32[]{:S(2)}, u32[]{:S(2)}) async-start(bf16[16,512,128]{2,1,0:T(8,128)(2,1)} %get-tuple-element.25), calls=%async_computation | async-start | bytes 4194304 | tf_op jit(solution)/shard_map/all_to_all | solution.py:532
  17.2 25.9 %copy-start = (s32[4096]{0:T(1024)S(1)}, s32[4096]{0:T(1024)}, u32[]{:S(2)}) copy-start(s32[4096]{0:T(1024)} %get-tuple-element.24.flat_ref) | copy-start | bytes 49156
  17.3 25.9 %copy-start.1 = (f32[1024]{0:T(1024)S(1)}, f32[1024]{0:T(1024)}, u32[]{:S(2)}) copy-start(f32[1024]{0:T(1024)} %param.25) | copy-start | bytes 12292
  17.3 25.9 %copy-start.2 = (f32[512]{0:T(512)S(1)}, f32[512]{0:T(512)}, u32[]{:S(2)}) copy-start(f32[512]{0:T(512)} %param.21) | copy-start | bytes 6148
  17.3 25.9 %copy-start.3 = (f32[512]{0:T(512)S(1)}, f32[512]{0:T(512)}, u32[]{:S(2)}) copy-start(f32[512]{0:T(512)} %param.23) | copy-start | bytes 6148
  43.1 10.5 %copy-start.4 = (s32[16]{0:T(128)S(1)}, s32[16]{0:T(128)}, u32[]{:S(2)}) copy-start(s32[16]{0:T(128)} %reach_ref.3) | copy-start | bytes 196
  51.5 11.2 %collective-permute-start = (bf16[128,1024]{1,0:T(8,128)(2,1)S(1)}, bf16[128,1024]{1,0:T(8,128)(2,1)S(1)}, u32[]{:S(2)}, u32[]{:S(2)}) collective-permute-start(bf16[128,1024]{1,0:T(8,128)(2,1)S(1)} %get-tuple-element.34), channel_id=1, source_target_pairs={{0,15},{1,0},{2,1},{3,2},{4,3},{5,4},{6,5},{7,6},{8,7},{9,8},{10,9... | collective-permute-start | bytes 786440 | tf_op jit(solution)/shard_map/ppermute | solution.py:601
  52.4 10.3 %collective-permute-start.1 = (bf16[128,1024]{1,0:T(8,128)(2,1)S(1)}, bf16[128,1024]{1,0:T(8,128)(2,1)S(1)}, u32[]{:S(2)}, u32[]{:S(2)}) collective-permute-start(bf16[128,1024]{1,0:T(8,128)(2,1)S(1)} %get-tuple-element.35), channel_id=1, source_target_pairs={{0,1},{1,2},{2,3},{3,4},{4,5},{5,6},{6,7},{7,8},{8,9},{9,10},{10,1... | collective-permute-start | bytes 786440 | tf_op jit(solution)/shard_map/ppermute | solution.py:600
